TPU v7x, 128 devices: a whole 4x4x4 slice. The times are simulated.
128 devices in a mesh: dp: 8 (over y_lo, z), mp: 16 (over x, y_hi, core).
Axes of the slice: x: 4, y: 4 (y_hi: 2, y_lo: 2; y = y_hi * 2 + y_lo), z: 4, core: 2. Of those that a mesh axis runs over, the one named last changes fastest.
Arguments:
- tokens: bfloat16 [128, 256, 1280], P(('dp', 'mp'))
- slot_keys: bfloat16 [256, 1280], P(('dp', 'mp'))
- weight_in: bfloat16 [128, 1280, 2560], P(('dp', 'mp')), may hold values from -0.15625 to 0.15625
- weight_out: bfloat16 [128, 2560, 1280], P(('dp', 'mp')), may hold values from -0.125 to 0.125
- cotangent: bfloat16 [128, 256, 1280], P(('dp', 'mp')), may hold values from -6 to 6
Outputs:
- mixed_out: bfloat16 [128, 256, 1280], P(('dp', 'mp'))
- grad_tokens: bfloat16 [128, 256, 1280], P(('dp', 'mp'))
- grad_keys: float32 [256, 1280], P(('dp', 'mp'))
- grad_w_out: bfloat16 [128, 2560, 1280], P(('dp', 'mp'))
All inputs are finite; a program needn't handle non-finite values.
Results may differ from a plain program's by a relative error of at most 0.01.
Values may be sent and summed in bfloat16 or wider, within the bound.
No kernel may reach another device: no remote copies, remote signals or barrier semaphores. Data moves between devices by JAX's collectives and lax.ppermute only.
A program may use at most 128 MiB of HBM per device.

v0:
```python
import jax
import jax.numpy as jnp
from jax import lax
from jax.sharding import PartitionSpec as P

SLOTS_EXP = 2


inv_root_two = 0.7071067811865476
inv_root_tau = 0.3989422804014327


def gelu_pair(values):
    cumulative = 0.5 * (1.0 + jax.scipy.special.erf(values * inv_root_two))
    density = jnp.exp(-0.5 * values * values) * inv_root_tau
    return (values * cumulative, cumulative + values * density)


def move_slots(blocks):
    return lax.all_to_all(blocks, ("dp", "mp"), split_axis=0, concat_axis=0, tiled=True)


def local(tokens, slot_keys, weight_in, weight_out, cotangent):
    keys_all = lax.all_gather(slot_keys, ("dp", "mp"), axis=0, tiled=True)
    images_here, length, feature_width = tokens.shape
    experts = keys_all.shape[0] // SLOTS_EXP
    logits = jnp.einsum("itd,sd->its", tokens, keys_all, preferred_element_type=jnp.float32)
    dispatch = jax.nn.softmax(logits, axis=1)
    combine = jax.nn.softmax(logits, axis=2)
    split_shape = (images_here, length, experts, SLOTS_EXP)
    dispatch_low = dispatch.astype(jnp.bfloat16).reshape(split_shape)
    combine_low = combine.astype(jnp.bfloat16).reshape(split_shape)
    slots_in = jnp.einsum(
        "itek,itd->eikd", dispatch_low, tokens, preferred_element_type=jnp.float32
    ).astype(jnp.bfloat16)
    arrived = move_slots(slots_in)
    slot_rows = arrived.reshape(-1, feature_width)
    first_weight = weight_in[0]
    second_weight = weight_out[0]
    pre_act = jnp.dot(slot_rows, first_weight, preferred_element_type=jnp.float32)
    active, gelu_slope = gelu_pair(pre_act)
    hidden = active.astype(jnp.bfloat16)
    expert_out = jnp.dot(hidden, second_weight, preferred_element_type=jnp.float32).astype(
        jnp.bfloat16
    )
    slot_out = move_slots(expert_out.reshape(arrived.shape))
    mixed_out = jnp.einsum(
        "itek,eikd->itd", combine_low, slot_out, preferred_element_type=jnp.float32
    ).astype(jnp.bfloat16)
    grad_combine = jnp.einsum(
        "itd,eikd->itek", cotangent, slot_out, preferred_element_type=jnp.float32
    ).reshape(logits.shape)
    grad_slot_out = jnp.einsum(
        "itek,itd->eikd", combine_low, cotangent, preferred_element_type=jnp.float32
    ).astype(jnp.bfloat16)
    grad_rows = move_slots(grad_slot_out).reshape(-1, feature_width)
    grad_second = jnp.dot(hidden.T, grad_rows, preferred_element_type=jnp.float32).astype(
        jnp.bfloat16
    )
    grad_hidden = jnp.dot(grad_rows, second_weight.T, preferred_element_type=jnp.float32)
    grad_pre = (grad_hidden * gelu_slope).astype(jnp.bfloat16)
    grad_rows_in = jnp.dot(grad_pre, first_weight.T, preferred_element_type=jnp.float32).astype(
        jnp.bfloat16
    )
    grad_slot_in = move_slots(grad_rows_in.reshape(arrived.shape))
    grad_dispatch = jnp.einsum(
        "itd,eikd->itek", tokens, grad_slot_in, preferred_element_type=jnp.float32
    ).reshape(logits.shape)
    grad_logits = dispatch * (
        grad_dispatch - jnp.sum(dispatch * grad_dispatch, axis=1, keepdims=True)
    ) + combine * (grad_combine - jnp.sum(combine * grad_combine, axis=2, keepdims=True))
    grad_low = grad_logits.astype(jnp.bfloat16)
    through_slots = jnp.einsum(
        "itek,eikd->itd", dispatch_low, grad_slot_in, preferred_element_type=jnp.float32
    )
    through_keys = jnp.einsum("its,sd->itd", grad_low, keys_all, preferred_element_type=jnp.float32)
    grad_tokens = (through_slots + through_keys).astype(jnp.bfloat16)
    key_terms = jnp.einsum("its,itd->sd", grad_low, tokens, preferred_element_type=jnp.float32)
    grad_keys = lax.psum_scatter(key_terms, ("dp", "mp"), scatter_dimension=0, tiled=True)
    return (mixed_out, grad_tokens, grad_keys, grad_second[None])


def solution(mesh):
    in_specs = (
        P(("dp", "mp"), None, None),
        P(("dp", "mp"), None),
        P(("dp", "mp"), None, None),
        P(("dp", "mp"), None, None),
        P(("dp", "mp"), None, None),
    )
    out_specs = (
        P(("dp", "mp"), None, None),
        P(("dp", "mp"), None, None),
        P(("dp", "mp"), None),
        P(("dp", "mp"), None, None),
    )
    return jax.shard_map(local, mesh=mesh, in_specs=in_specs, out_specs=out_specs, check_vma=False)
```

profile of v0, /device:TPU:1, one launch (start us, length us, event | category | flops | bytes accessed | tf_op | source)
XLA Modules:
  0.0 432.2 jit_solution(12663078052494656327)
XLA Ops:
  7.2 0.0 copy-start
  7.2 182.3 %all-gather = bf16[128,2,1280]{2,1,0:T(2,128)(2,1)S(1)} all-gather(bf16[1,2,1280]{2,1,0:T(2,128)(2,1)} %bitcast.96), channel_id=1, replica_groups=mesh['dp'=8,'mp'=16] {'dp','mp'}, dimensions={0}, use_global_device_ids=true | all-gather | bytes 660480 | tf_op jit(solution)/shard_map/all_gather | solution.py:24
  189.5 0.2 reshape.142
  189.7 0.0 copy-done
  189.8 0.5 fusion.59
  190.2 0.2 fusion.50
  190.4 0.0 copy-start.3
  190.4 0.1 fusion.57
  190.6 0.1 reshape.131
  190.6 0.1 copy.36
  190.8 0.4 fusion.27
  191.2 1.5 copy.28
  192.7 3.6 all-to-all-start
  196.3 0.1 reshape.130
  196.3 0.0 copy-done.3
  196.3 0.0 copy-start.1
  196.3 0.3 fusion.28
  196.7 1.5 copy.33
  198.2 13.1 %all-to-all-done = bf16[128,1,2,1280]{3,2,1,0:T(2,128)(2,1)S(1)} async-done(((bf16[128,1,2,1280]{3,2,1,0:T(2,128)(2,1)}), bf16[128,1,2,1280]{3,2,1,0:T(2,128)(2,1)S(1)}, u32[]{:S(2)}, u32[]{:S(2)}) %all-to-all-start) | async-done | bytes 655392 | tf_op jit(solution)/shard_map/all_to_all | solution.py:20
  211.3 0.0 copy-done.1
  211.3 4.2 all-to-all-start.2
  215.6 1.1 reshape.132
  216.7 4.9 %fusion.7 = f32[256,2560]{1,0:T(8,128)S(1)} fusion(bf16[256,1280]{1,0:T(8,128)(2,1)} %reshape.132, bf16[1,1280,2560]{2,1,0:T(8,128)(2,1)} %param.7), kind=kOutput, calls=%fused_computation.8 | convolution fusion | flops 1677721600 | bytes 9830400 | tf_op jit(solution)/shard_map/dot_general | solution.py:40
  221.6 0.0 copy-start.8
  221.6 1.5 copy-done.8
  223.1 4.9 %fusion.22 = bf16[256,1280]{1,0:T(8,128)(2,1)S(1)} fusion(bf16[1,2560,1280]{2,1,0:T(8,128)(2,1)} %param.8, f32[256,2560]{1,0:T(8,128)S(1)} %fusion.7), kind=kOutput, calls=%fused_computation.23 | convolution fusion | flops 1681326080 | bytes 9830400 | tf_op jit(solution)/shard_map/dot_general | solution.py:43
  228.0 1.1 reshape.133
  229.1 1.4 all-to-all-done.2
  230.5 8.4 %all-to-all-start.1 = ((bf16[128,1,2,1280]{3,2,1,0:T(2,128)(2,1)}), bf16[128,1,2,1280]{3,2,1,0:T(2,128)(2,1)S(1)}, u32[]{:S(2)}, u32[]{:S(2)}) async-start(bf16[128,1,2,1280]{3,2,1,0:T(2,128)(2,1)} %bitcast.8), calls=%async_computation.1 | async-start | bytes 1310720 | tf_op jit(solution)/shard_map/all_to_all | solution.py:20
  238.9 1.1 reshape.136
  239.9 9.4 %fusion.19 = bf16[256,1280]{1,0:T(8,128)(2,1)S(1)} fusion(bf16[1,1280,2560]{2,1,0:T(8,128)(2,1)} %param.7, bf16[256,1280]{1,0:T(8,128)(2,1)} %reshape.136, bf16[1,2560,1280]{2,1,0:T(8,128)(2,1)} %param.8, f32[256,2560]{1,0:T(8,128)} %copy-done.8), kind=kOutput, calls=%fused_computation.22 | convolution fusion | flops 3362324480 | bytes 17039360 | tf_op jit(solution)/shard_map/dot_general | solution.py:62
  249.3 1.1 reshape.137
  250.4 3.3 all-to-all-done.1
  253.8 6.4 %all-to-all-start.3 = ((bf16[128,1,2,1280]{3,2,1,0:T(2,128)(2,1)}), bf16[128,1,2,1280]{3,2,1,0:T(2,128)(2,1)S(1)}, u32[]{:S(2)}, u32[]{:S(2)}) async-start(bf16[128,1,2,1280]{3,2,1,0:T(2,128)(2,1)} %bitcast.17), calls=%async_computation.3 | async-start | bytes 1310720 | tf_op jit(solution)/shard_map/all_to_all | solution.py:20
  260.2 0.0 all-reduce.3.cloned.1.call-start
  260.2 1.5 convolution_bitcast_fusion.2
  261.7 0.2 copy.38
  261.9 0.2 reshape.140
  262.1 13.0 %all-to-all-done.3 = bf16[128,1,2,1280]{3,2,1,0:T(2,128)(2,1)S(1)} async-done(((bf16[128,1,2,1280]{3,2,1,0:T(2,128)(2,1)}), bf16[128,1,2,1280]{3,2,1,0:T(2,128)(2,1)S(1)}, u32[]{:S(2)}, u32[]{:S(2)}) %all-to-all-start.3) | async-done | bytes 655392 | tf_op jit(solution)/shard_map/all_to_all | solution.py:20
  275.1 0.4 convolution_bitcast_fusion.3
  275.5 0.9 copy.37
  276.4 1.1 reshape.139
  277.5 0.2 multiply_reduce_fusion.1
  277.8 0.0 copy-start.4
  277.8 0.0 copy-start.6
  277.8 0.5 copy-done.4
  278.3 0.0 copy-done.6
  278.3 1.5 fusion.41
  279.8 0.0 all-reduce.3.cloned.1.call-update
  279.9 0.0 copy-start.2
  279.9 7.0 %fusion = bf16[1,2560,1280]{2,1,0:T(8,128)(2,1)} fusion(bf16[256,1280]{1,0:T(8,128)(2,1)} %reshape.136, f32[256,2560]{1,0:T(8,128)} %copy-done.8), kind=kOutput, calls=%fused_computation.1 | convolution fusion | flops 1684275200 | bytes 9830400 | tf_op jit(solution)/shard_map/dot_general | solution.py:57
  286.8 0.0 copy-start.5
  286.8 0.0 copy-start.7
  286.8 0.3 convolution_bitcast_fusion
  287.2 0.0 copy-done.2
  287.2 1.2 fusion.30
  288.4 0.0 copy-done.5
  288.4 0.0 copy-done.7
  288.4 1.4 fusion.29
  289.8 134.2 %all-reduce.3.cloned.1.call-done = f32[256,1280]{1,0:T(8,128)} async-done(((f32[256,1280]{1,0:T(8,128)}), f32[256,1280]{1,0:T(8,128)}) %all-reduce.3.cloned.1.call-update) | async-done | bytes 1310736
  424.0 1.4 constant_dynamic-slice_fusion
Async XLA Ops:
  7.2 182.6 %copy-start = (bf16[1,256,1280]{2,1,0:T(8,128)(2,1)S(1)}, bf16[1,256,1280]{2,1,0:T(8,128)(2,1)}, u32[]{:S(2)}) copy-start(bf16[1,256,1280]{2,1,0:T(8,128)(2,1)} %param.5) | copy-start | bytes 1966084
  190.4 5.9 %copy-start.3 = (bf16[1,256,1280]{2,1,0:T(8,128)(2,1)S(1)}, bf16[1,256,1280]{2,1,0:T(8,128)(2,1)}, u32[]{:S(2)}) copy-start(bf16[1,256,1280]{2,1,0:T(8,128)(2,1)} %param.9) | copy-start | bytes 1966084
  192.7 18.6 %all-to-all-start = ((bf16[128,1,2,1280]{3,2,1,0:T(2,128)(2,1)}), bf16[128,1,2,1280]{3,2,1,0:T(2,128)(2,1)S(1)}, u32[]{:S(2)}, u32[]{:S(2)}) async-start(bf16[128,1,2,1280]{3,2,1,0:T(2,128)(2,1)} %copy.28), calls=%async_computation | async-start | bytes 1310720 | tf_op jit(solution)/shard_map/all_to_all | solution.py:20
  196.3 15.0 %copy-start.1 = (bf16[256,128,2]{0,2,1:T(2,128)(2,1)}, bf16[256,128,2]{0,2,1:T(2,128)(2,1)S(1)}, u32[]{:S(2)}) copy-start(bf16[256,128,2]{0,2,1:T(2,128)(2,1)S(1)} %reshape.130) | copy-start | bytes 393220
  211.3 19.2 %all-to-all-start.2 = ((bf16[128,1,2,1280]{3,2,1,0:T(2,128)(2,1)}), bf16[128,1,2,1280]{3,2,1,0:T(2,128)(2,1)S(1)}, u32[]{:S(2)}, u32[]{:S(2)}) async-start(bf16[128,1,2,1280]{3,2,1,0:T(2,128)(2,1)} %copy.33), calls=%async_computation.2 | async-start | bytes 1310720 | tf_op jit(solution)/shard_map/all_to_all | solution.py:20
  221.6 1.5 copy-start.8
  230.5 23.3 %all-to-all-start.1 = ((bf16[128,1,2,1280]{3,2,1,0:T(2,128)(2,1)}), bf16[128,1,2,1280]{3,2,1,0:T(2,128)(2,1)S(1)}, u32[]{:S(2)}, u32[]{:S(2)}) async-start(bf16[128,1,2,1280]{3,2,1,0:T(2,128)(2,1)} %bitcast.8), calls=%async_computation.1 | async-start | bytes 1310720 | tf_op jit(solution)/shard_map/all_to_all | solution.py:20
  253.8 21.4 %all-to-all-start.3 = ((bf16[128,1,2,1280]{3,2,1,0:T(2,128)(2,1)}), bf16[128,1,2,1280]{3,2,1,0:T(2,128)(2,1)S(1)}, u32[]{:S(2)}, u32[]{:S(2)}) async-start(bf16[128,1,2,1280]{3,2,1,0:T(2,128)(2,1)} %bitcast.17), calls=%async_computation.3 | async-start | bytes 1310720 | tf_op jit(solution)/shard_map/all_to_all | solution.py:20
  260.2 163.8 %all-reduce.3.cloned.1.call-start = ((), (), s32[]{:S(2)}) async-start(), calls=%async_computation.4 | async-start | bytes 2621440
  277.8 0.6 copy-start.4
  277.8 0.6 copy-start.6
  279.9 7.3 %copy-start.2 = (bf16[256,128,2]{0,2,1:T(2,128)(2,1)S(1)}, bf16[256,128,2]{0,2,1:T(2,128)(2,1)}, u32[]{:S(2)}) copy-start(bf16[256,128,2]{0,2,1:T(2,128)(2,1)} %copy-done.1) | copy-start | bytes 393220
  286.8 1.6 copy-start.5
  286.8 1.6 copy-start.7
Sparse Core Ops, SparseCore 0:
  280.0 143.9 all-reduce.2
where the time goes:
time: 433 us; the launch traced here: 432 us
  blocking collectives  182 us (42%)
  waiting for transfers between devices  165 us (38%)
  matrix products  33.6 us (8%)
  starting transfers between devices  22.7 us (5%)
  between operations  14.3 us (3%)
  local copies, waits for them, and re-layouts  13.7 us (3%)
    all_gather x1, blocking collectives, local(): keys_all = lax.all_gather(slot_keys, ('dp', 'mp'), axis=0, tiled=True)  182 us
    unnamed x2, waiting for transfers between devices  134 us
    all_to_all x4, waiting for transfers between devices, move_slots(): lax.all_to_all(blocks, ('dp', 'mp'), split_axis=0, concat_axis=0, tiled=T...  30.8 us
    all_to_all x4, starting transfers between devices, move_slots(): lax.all_to_all(blocks, ('dp', 'mp'), split_axis=0, concat_axis=0, tiled=T...  22.6 us
    dot_general x1, matrix products, local(): jnp.dot(grad_pre, first_weight.T, preferred_element_type=jnp.float32)  9.39 us
  transfers between devices with their start and end apart: 5, of which 5 were waited for; matrix products, arithmetic and copies ran while one was open for 9% of the time, Pallas kernels for 0%

commit v1 on v0

v1 whole, which is shorter than its diff:
```python
import jax
import jax.numpy as jnp
from jax import lax
from jax.sharding import PartitionSpec as P

SLOTS_EXP = 2
AXES = ("dp", "mp")

inv_root_two = 0.7071067811865476
inv_root_tau = 0.3989422804014327


def gelu_pair(values):
    cumulative = 0.5 * (1.0 + jax.scipy.special.erf(values * inv_root_two))
    density = jnp.exp(-0.5 * values * values) * inv_root_tau
    return (values * cumulative, cumulative + values * density)


def exchange(blocks):
    return lax.all_to_all(blocks, AXES, split_axis=0, concat_axis=0, tiled=True)


def dot(a, b, dims):
    return lax.dot_general(a, b, (dims, ((), ())), preferred_element_type=jnp.float32)


def local(tokens, slot_keys, weight_in, weight_out, cotangent):
    low = jnp.bfloat16
    devices = lax.axis_size(AXES)
    length, width = tokens.shape[1:]
    tokens, cotangent = tokens[0], cotangent[0]
    first_weight, second_weight = weight_in[0], weight_out[0]
    keys_all = exchange(jnp.broadcast_to(slot_keys[None], (devices, SLOTS_EXP, width)))
    keys_all = keys_all.reshape(-1, width)
    slots = keys_all.shape[0]

    logits = dot(tokens, keys_all, ((1,), (1,)))
    dispatch = jax.nn.softmax(logits, axis=0)
    combine = jax.nn.softmax(logits, axis=1)
    dispatch_low = dispatch.astype(low)
    combine_low = combine.astype(low)
    slots_in = dot(dispatch_low, tokens, ((0,), (0,))).astype(low)
    grad_slot_out = dot(combine_low, cotangent, ((0,), (0,))).astype(low)
    parts = (devices, SLOTS_EXP, width)
    arrived = exchange(
        jnp.concatenate([slots_in.reshape(parts), grad_slot_out.reshape(parts)], axis=1)
    )
    slot_rows = arrived[:, :SLOTS_EXP].reshape(-1, width)
    grad_rows = arrived[:, SLOTS_EXP:].reshape(-1, width)

    pre_act = dot(slot_rows, first_weight, ((1,), (0,)))
    active, gelu_slope = gelu_pair(pre_act)
    hidden = active.astype(low)
    expert_out = dot(hidden, second_weight, ((1,), (0,))).astype(low)
    grad_hidden = dot(grad_rows, second_weight, ((1,), (1,)))
    grad_pre = (grad_hidden * gelu_slope).astype(low)
    grad_rows_in = dot(grad_pre, first_weight, ((1,), (1,))).astype(low)
    back = exchange(
        jnp.concatenate([expert_out.reshape(parts), grad_rows_in.reshape(parts)], axis=1)
    )
    grad_second = dot(hidden, grad_rows, ((0,), (0,))).astype(low)
    slot_out = back[:, :SLOTS_EXP].reshape(slots, width)
    grad_slot_in = back[:, SLOTS_EXP:].reshape(slots, width)

    grad_combine = dot(cotangent, slot_out, ((1,), (1,)))
    grad_dispatch = dot(tokens, grad_slot_in, ((1,), (1,)))
    grad_logits = dispatch * (
        grad_dispatch - jnp.sum(dispatch * grad_dispatch, axis=0, keepdims=True)
    ) + combine * (grad_combine - jnp.sum(combine * grad_combine, axis=1, keepdims=True))
    grad_low = grad_logits.astype(low)
    key_terms = dot(grad_low, tokens, ((0,), (0,))).astype(low)
    key_parts = exchange(key_terms.reshape(parts))
    mixed_out = dot(combine_low, slot_out, ((1,), (0,))).astype(low)
    through_slots = dot(dispatch_low, grad_slot_in, ((1,), (0,)))
    through_keys = dot(grad_low, keys_all, ((1,), (0,)))
    grad_tokens = (through_slots + through_keys).astype(low)
    grad_keys = jnp.sum(key_parts.astype(jnp.float32), axis=0)
    return (mixed_out[None], grad_tokens[None], grad_keys, grad_second[None])


def solution(mesh):
    in_specs = (
        P(AXES, None, None),
        P(AXES, None),
        P(AXES, None, None),
        P(AXES, None, None),
        P(AXES, None, None),
    )
    out_specs = (
        P(AXES, None, None),
        P(AXES, None, None),
        P(AXES, None),
        P(AXES, None, None),
    )
    return jax.shard_map(local, mesh=mesh, in_specs=in_specs, out_specs=out_specs, check_vma=False)
```

time: 433 us -> 140 us (0.32)
  waiting for transfers between devices: 165 us -> 27.2 us
  blocking collectives: 182 us -> 52.1 us
  starting transfers between devices: 22.7 us -> 8.61 us
  between operations: 14.3 us -> 0.85 us
  other arithmetic: 0.56 us -> 5.34 us
    all_gather x1 -> x0, blocking collectives: 182 us -> none  [local(): keys_all = lax.all_gather(slot_keys, ('dp', 'mp'), axis=0, tiled=True)]
    unnamed x2 -> x0, waiting for transfers between devices: 134 us -> none
    all_to_all x0 -> x2, blocking collectives: none -> 52.1 us  [exchange(): return lax.all_to_all(blocks, AXES, split_axis=0, concat_axis=0, tiled=True)]
    all_to_all x4 -> x2, starting transfers between devices: 22.6 us -> 8.61 us  [exchange(): return lax.all_to_all(blocks, AXES, split_axis=0, concat_axis=0, tiled=True)]
    all_to_all x4 -> x2, waiting for transfers between devices: 30.8 us -> 27.2 us  [exchange(): return lax.all_to_all(blocks, AXES, split_axis=0, concat_axis=0, tiled=True)]
  transfers between devices with their start and end apart: 5 -> 2, of which waited for: 5 -> 2; matrix products, arithmetic and copies ran while one was open for 9% -> 7% of each run, Pallas kernels for 0% -> 0%
where the time goes in v1:
time: 140 us; the launch traced here: 139 us
  blocking collectives  52.1 us (37%)
  matrix products  31.5 us (22%)
  waiting for transfers between devices  27.2 us (19%)
  local copies, waits for them, and re-layouts  13.6 us (10%)
  starting transfers between devices  8.61 us (6%)
  other arithmetic  5.34 us (4%)
    all_to_all x2, blocking collectives, exchange(): return lax.all_to_all(blocks, AXES, split_axis=0, concat_axis=0, tiled=True)  52.1 us
    dot_general x13, matrix products, dot(): lax.dot_general(a, b, (dims, ((), ())), preferred_element_type=jnp.float32)  31.5 us
    all_to_all x2, waiting for transfers between devices, exchange(): return lax.all_to_all(blocks, AXES, split_axis=0, concat_axis=0, tiled=True)  27.2 us
    all_to_all x2, starting transfers between devices, exchange(): return lax.all_to_all(blocks, AXES, split_axis=0, concat_axis=0, tiled=True)  8.61 us
  transfers between devices with their start and end apart: 2, of which 2 were waited for; matrix products, arithmetic and copies ran while one was open for 7% of the time, Pallas kernels for 0%

profile of v1, /device:TPU:1, one launch (start us, length us, event | category | flops | bytes accessed | tf_op | source)
XLA Modules:
  0.0 139.2 jit_solution(4000307633563461796)
XLA Ops:
  0.6 0.0 copy-start
  0.6 1.1 broadcast_in_dim.8
  1.7 26.2 %all_to_all.20 = bf16[128,2,1280]{2,1,0:T(2,128)(2,1)S(1)} all-to-all(bf16[128,2,1280]{2,1,0:T(2,128)(2,1)S(1)} %broadcast_in_dim.8), channel_id=1, replica_groups=mesh['dp'=8,'mp'=16] {'dp','mp'}, dimensions={0} | all-to-all | bytes 1310720 | tf_op jit(solution)/shard_map/all_to_all | solution.py:20
  28.0 0.2 reshape.45
  28.2 0.0 copy-done
  28.2 0.0 copy-start.3
  28.2 0.4 fusion.52
  28.7 0.2 fusion.40
  28.9 0.4 convolution_convert_fusion.4
  29.3 0.2 reshape.46
  29.5 0.0 copy-done.3
  29.5 0.5 convolution_convert_fusion.3
  30.1 0.2 reshape.47
  30.3 1.4 pad_maximum_fusion
  31.7 25.9 %all_to_all.21 = bf16[128,4,1280]{2,1,0:T(4,128)(2,1)S(1)} all-to-all(bf16[128,4,1280]{2,1,0:T(4,128)(2,1)S(1)} %pad_maximum_fusion), channel_id=1, replica_groups=mesh['dp'=8,'mp'=16] {'dp','mp'}, dimensions={0} | all-to-all | bytes 2621440 | tf_op jit(solution)/shard_map/all_to_all | solution.py:20
  57.6 0.9 fusion.54
  58.5 1.1 reshape.48
  59.6 0.2 reshape.50
  59.8 4.9 %fusion.7 = f32[256,2560]{1,0:T(8,128)S(1)} fusion(bf16[256,1280]{1,0:T(8,128)(2,1)} %reshape.48, bf16[1,1280,2560]{2,1,0:T(8,128)(2,1)} %param.7), kind=kOutput, calls=%fused_computation.8 | convolution fusion | flops 1677721600 | bytes 9830400 | tf_op jit(solution)/shard_map/dot_general | solution.py:24
  64.8 0.0 copy-start.4
  64.8 1.5 %copy-done.4 = f32[256,2560]{1,0:T(8,128)} copy-done((f32[256,2560]{1,0:T(8,128)}, f32[256,2560]{1,0:T(8,128)S(1)}, u32[]{:S(2)}) %copy-start.4) | copy-done | bytes 2621464
  66.3 4.9 %fusion.22 = bf16[256,1280]{1,0:T(8,128)(2,1)S(1)} fusion(bf16[1,2560,1280]{2,1,0:T(8,128)(2,1)} %param.8, f32[256,2560]{1,0:T(8,128)S(1)} %fusion.7), kind=kOutput, calls=%fused_computation.21 | convolution fusion | flops 1681326080 | bytes 9830400 | tf_op jit(solution)/shard_map/dot_general | solution.py:24
  71.2 0.2 reshape.49
  71.4 8.5 %fusion.19 = bf16[256,1280]{1,0:T(8,128)(2,1)} fusion(bf16[1,1280,2560]{2,1,0:T(8,128)(2,1)} %param.7, bf16[256,1280]{1,0:T(8,128)(2,1)S(1)} %reshape.50, bf16[1,2560,1280]{2,1,0:T(8,128)(2,1)} %param.8, f32[256,2560]{1,0:T(8,128)} %copy-done.4), kind=kOutput, calls=%fused_computation.20 | convolution fusion | flops 3362324480 | bytes 17039360 | tf_op jit(solution)/shard_map/dot_general | solution.py:24
  79.9 2.0 %reshape.51 = bf16[128,2,1280]{2,1,0:T(2,128)(2,1)S(1)} reshape(bf16[256,1280]{1,0:T(8,128)(2,1)} %fusion.19) | data formatting | bytes 1310720 | tf_op jit(solution)/shard_map/reshape | solution.py:59
  81.9 2.4 %pad_maximum_fusion.1 = bf16[128,4,1280]{2,1,0:T(4,128)(2,1)} fusion(bf16[128,2,1280]{2,1,0:T(2,128)(2,1)S(1)} %reshape.51, bf16[128,2,1280]{2,1,0:T(2,128)(2,1)S(1)} %reshape.49), kind=kLoop, calls=%fused_computation.30 | loop fusion | flops 2621440 | bytes 2621440 | tf_op jit(solution)/shard_map/concatenate | solution.py:59
  84.3 4.3 %all-to-all-start.2 = ((bf16[128,4,1280]{2,1,0:T(4,128)(2,1)}), bf16[128,4,1280]{2,1,0:T(4,128)(2,1)S(1)}, u32[]{:S(2)}, u32[]{:S(2)}) async-start(bf16[128,4,1280]{2,1,0:T(4,128)(2,1)} %pad_maximum_fusion.1), calls=%async_computation.2 | async-start | bytes 2621440 | tf_op jit(solution)/shard_map/all_to_all | solution.py:20
  88.7 6.8 %fusion = bf16[1,2560,1280]{2,1,0:T(8,128)(2,1)} fusion(bf16[256,1280]{1,0:T(8,128)(2,1)S(1)} %reshape.50, f32[256,2560]{1,0:T(8,128)} %copy-done.4), kind=kOutput, calls=%fused_computation.1 | convolution fusion | flops 1684275200 | bytes 9830400 | tf_op jit(solution)/shard_map/dot_general | solution.py:24
  95.5 15.1 %all-to-all-done.2 = bf16[128,4,1280]{2,1,0:T(4,128)(2,1)S(1)} async-done(((bf16[128,4,1280]{2,1,0:T(4,128)(2,1)}), bf16[128,4,1280]{2,1,0:T(4,128)(2,1)S(1)}, u32[]{:S(2)}, u32[]{:S(2)}) %all-to-all-start.2) | async-done | bytes 1310752 | tf_op jit(solution)/shard_map/all_to_all | solution.py:20
  110.5 1.7 %fusion.53 = (bf16[128,2,1280]{2,1,0:T(2,128)(2,1)}, bf16[128,2,1280]{2,1,0:T(2,128)(2,1)S(1)}) fusion(bf16[128,4,1280]{2,1,0:T(4,128)(2,1)S(1)} %all-to-all-done.2), kind=kLoop, calls=%fused_computation.58 | loop fusion | bytes 2621440 | tf_op jit(solution)/shard_map/slice | solution.py:63
  112.3 2.1 %reshape.53 = bf16[256,1280]{1,0:T(8,128)(2,1)S(1)} reshape(bf16[128,2,1280]{2,1,0:T(2,128)(2,1)} %get-tuple-element.10) | data formatting | bytes 1310720 | tf_op jit(solution)/shard_map/reshape | solution.py:63
  114.3 0.2 reshape.52
  114.6 1.5 %convolution_bitcast_fusion = f32[256,256]{1,0:T(8,128)S(1)} fusion(bf16[256,1280]{1,0:T(8,128)(2,1)S(1)} %reshape.52, bf16[1,256,1280]{2,1,0:T(8,128)(2,1)} %param.9), kind=kOutput, calls=%fused_computation.32 | convolution fusion | flops 167772160 | bytes 1572864 | tf_op jit(solution)/shard_map/dot_general | solution.py:24
  116.1 0.4 multiply_reduce_fusion.1
  116.5 0.2 add_convert_fusion
  116.7 0.0 copy-start.1
  116.7 0.6 copy-done.1
  117.3 0.4 convolution_convert_fusion.1
  117.7 1.1 reshape.54
  118.8 4.3 %all-to-all-start.3 = ((bf16[128,2,1280]{2,1,0:T(2,128)(2,1)}), bf16[128,2,1280]{2,1,0:T(2,128)(2,1)S(1)}, u32[]{:S(2)}, u32[]{:S(2)}) async-start(bf16[128,2,1280]{2,1,0:T(2,128)(2,1)} %reshape.54), calls=%async_computation.3 | async-start | bytes 1310720 | tf_op jit(solution)/shard_map/all_to_all | solution.py:20
  123.1 0.0 copy-start.2
  123.1 1.2 fusion.26
  124.4 0.4 fusion.41
  124.7 0.0 copy-done.2
  124.7 1.2 fusion.27
  125.9 12.1 %all-to-all-done.3 = bf16[128,2,1280]{2,1,0:T(2,128)(2,1)S(1)} async-done(((bf16[128,2,1280]{2,1,0:T(2,128)(2,1)}), bf16[128,2,1280]{2,1,0:T(2,128)(2,1)S(1)}, u32[]{:S(2)}, u32[]{:S(2)}) %all-to-all-start.3) | async-done | bytes 655392 | tf_op jit(solution)/shard_map/all_to_all | solution.py:20
  138.0 1.2 convert_reduce_fusion
Async XLA Ops:
  0.6 27.6 %copy-start = (bf16[1,256,1280]{2,1,0:T(8,128)(2,1)S(1)}, bf16[1,256,1280]{2,1,0:T(8,128)(2,1)}, u32[]{:S(2)}) copy-start(bf16[1,256,1280]{2,1,0:T(8,128)(2,1)} %param.5) | copy-start | bytes 1966084
  28.2 1.3 copy-start.3
  64.8 1.5 %copy-start.4 = (f32[256,2560]{1,0:T(8,128)}, f32[256,2560]{1,0:T(8,128)S(1)}, u32[]{:S(2)}) copy-start(f32[256,2560]{1,0:T(8,128)S(1)} %fusion.7) | copy-start | bytes 7864324
  84.3 26.2 %all-to-all-start.2 = ((bf16[128,4,1280]{2,1,0:T(4,128)(2,1)}), bf16[128,4,1280]{2,1,0:T(4,128)(2,1)S(1)}, u32[]{:S(2)}, u32[]{:S(2)}) async-start(bf16[128,4,1280]{2,1,0:T(4,128)(2,1)} %pad_maximum_fusion.1), calls=%async_computation.2 | async-start | bytes 2621440 | tf_op jit(solution)/shard_map/all_to_all | solution.py:20
  116.7 0.7 copy-start.1
  118.8 19.2 %all-to-all-start.3 = ((bf16[128,2,1280]{2,1,0:T(2,128)(2,1)}), bf16[128,2,1280]{2,1,0:T(2,128)(2,1)S(1)}, u32[]{:S(2)}, u32[]{:S(2)}) async-start(bf16[128,2,1280]{2,1,0:T(2,128)(2,1)} %reshape.54), calls=%async_computation.3 | async-start | bytes 1310720 | tf_op jit(solution)/shard_map/all_to_all | solution.py:20
  123.1 1.6 %copy-start.2 = (bf16[256,256]{1,0:T(8,128)(2,1)S(1)}, bf16[256,256]{1,0:T(8,128)(2,1)}, u32[]{:S(2)}) copy-start(bf16[256,256]{1,0:T(8,128)(2,1)} %copy-done.1) | copy-start | bytes 393220

commit v2 on v1

v2 whole, which is shorter than its diff:
```python
import jax
import jax.numpy as jnp
from jax import lax
from jax.experimental import pallas as pl
from jax.experimental.pallas import tpu as pltpu
from jax.sharding import PartitionSpec as P

SLOTS_EXP = 2
AXES = ("dp", "mp")
LOW = jnp.bfloat16
FF_BLOCK = 512
D_BLOCK = 256
MIB = 1 << 20

inv_root_two = 0.7071067811865476
inv_root_tau = 0.3989422804014327


def gelu_pair(values):
    cumulative = 0.5 * (1.0 + lax.erf(values * inv_root_two))
    density = jnp.exp(-0.5 * values * values) * inv_root_tau
    return (values * cumulative, cumulative + values * density)


def device_count():
    return lax.axis_size(AXES)


def exchange(blocks):
    return lax.all_to_all(blocks, AXES, split_axis=0, concat_axis=0, tiled=True)


def dot(a, b, dims):
    return lax.dot_general(a, b, (dims, ((), ())), preferred_element_type=jnp.float32)


def softmax(values, axis):
    powers = jnp.exp(values - jnp.max(values, axis=axis, keepdims=True))
    return powers / jnp.sum(powers, axis=axis, keepdims=True)


def route_kernel(tokens, cotangent, keys, send, dispatch_out, combine_out, keys_out):
    pairs = keys.shape[0]
    slots, width = keys_out.shape
    keys_out[...] = keys[...].reshape(slots, width)
    logits = dot(tokens[...], keys_out[...], ((1,), (1,)))
    dispatch = softmax(logits, 0)
    dispatch_out[...] = dispatch
    slots_in = dot(dispatch.astype(LOW), tokens[...], ((0,), (0,))).astype(LOW)
    send[:, 0] = slots_in.reshape(pairs, SLOTS_EXP, width)
    combine = softmax(logits, 1)
    combine_out[...] = combine
    grad_slot_out = dot(combine.astype(LOW), cotangent[...], ((0,), (0,))).astype(LOW)
    send[:, 1] = grad_slot_out.reshape(pairs, SLOTS_EXP, width)


def expert_kernel(
    arrived, first_hbm, second_hbm, send, hidden, grads, rows, grad_pre, first, second, sems
):
    width, inner = first.shape
    pairs = arrived.shape[0]
    steps = inner // FF_BLOCK
    copies = []
    for i in range(steps):
        block = pl.ds(i * FF_BLOCK, FF_BLOCK)
        copies.append(
            (
                pltpu.make_async_copy(first_hbm.at[:, block], first.at[:, block], sems.at[0, i]),
                pltpu.make_async_copy(second_hbm.at[block, :], second.at[block, :], sems.at[1, i]),
            )
        )
    for copy_in, copy_out in copies:
        copy_in.start()
        copy_out.start()
    rows[...] = arrived[:, 0].reshape(rows.shape)
    grads[...] = arrived[:, 1].reshape(rows.shape)
    for i in range(steps):
        block = pl.ds(i * FF_BLOCK, FF_BLOCK)
        copies[i][0].wait()
        pre_act = dot(rows[...], first[:, block], ((1,), (0,)))
        copies[i][1].wait()
        grad_hidden = dot(grads[...], second[block, :], ((1,), (1,)))
        active, slope = gelu_pair(pre_act)
        hidden[:, block] = active.astype(LOW)
        grad_pre[:, block] = (grad_hidden * slope).astype(LOW)
    for j in range(width // D_BLOCK):
        block = pl.ds(j * D_BLOCK, D_BLOCK)
        out = dot(hidden[...], second[:, block], ((1,), (0,))).astype(LOW)
        send[:, 0, :, block] = out.reshape(pairs, SLOTS_EXP, D_BLOCK)
        back = dot(grad_pre[...], first[block, :], ((1,), (1,))).astype(LOW)
        send[:, 1, :, block] = back.reshape(pairs, SLOTS_EXP, D_BLOCK)


def logit_kernel(
    back, tokens, cotangent, dispatch_in, combine_in, send, grad_low_out, slot_out, grad_slot_in
):
    slot_out[...] = back[:, 0].reshape(slot_out.shape)
    grad_slot_in[...] = back[:, 1].reshape(slot_out.shape)
    dispatch = dispatch_in[...]
    combine = combine_in[...]
    grad_combine = dot(cotangent[...], slot_out[...], ((1,), (1,)))
    grad_dispatch = dot(tokens[...], grad_slot_in[...], ((1,), (1,)))
    grad_logits = dispatch * (
        grad_dispatch - jnp.sum(dispatch * grad_dispatch, axis=0, keepdims=True)
    ) + combine * (grad_combine - jnp.sum(combine * grad_combine, axis=1, keepdims=True))
    grad_low = grad_logits.astype(LOW)
    grad_low_out[...] = grad_low
    terms = dot(grad_low, tokens[...], ((0,), (0,))).astype(LOW)
    send[...] = terms.reshape(send.shape)


def sum_kernel(terms, total):
    width = terms.shape[2]
    parts = terms[...].reshape(-1, 8, width).astype(jnp.float32)
    eight = jnp.sum(parts, axis=0)
    acc = eight[0:SLOTS_EXP]
    for i in range(1, 8 // SLOTS_EXP):
        acc = acc + eight[i * SLOTS_EXP : (i + 1) * SLOTS_EXP]
    total[...] = acc


VMEM = pl.BlockSpec(memory_space=pltpu.VMEM)
ANYWHERE = pl.BlockSpec(memory_space=pl.ANY)


def shaped(dtype, *shape):
    return jax.ShapeDtypeStruct(shape, dtype)


def local(tokens, slot_keys, weight_in, weight_out, cotangent):
    devices = device_count()
    length, width = tokens.shape[1:]
    inner = weight_in.shape[2]
    slots = devices * SLOTS_EXP
    tokens, cotangent = tokens[0], cotangent[0]
    first_weight, second_weight = weight_in[0], weight_out[0]
    pair_shape = (devices, SLOTS_EXP, width)
    twin_shape = (devices, 2, SLOTS_EXP, width)
    keys = exchange(jnp.broadcast_to(slot_keys[None], pair_shape))

    send, dispatch, combine, keys_all = pl.pallas_call(
        route_kernel,
        out_shape=[
            shaped(LOW, *twin_shape),
            shaped(jnp.float32, length, slots),
            shaped(jnp.float32, length, slots),
            shaped(LOW, slots, width),
        ],
        in_specs=[VMEM] * 3,
        out_specs=[VMEM] * 4,
        compiler_params=pltpu.CompilerParams(vmem_limit_bytes=32 * MIB),
        name="route",
    )(tokens, cotangent, keys)
    arrived = exchange(send)

    rows = arrived.shape[0] * SLOTS_EXP
    steps = inner // FF_BLOCK
    send, hidden, grads = pl.pallas_call(
        expert_kernel,
        out_shape=[
            shaped(LOW, *twin_shape),
            shaped(LOW, rows, inner),
            shaped(LOW, rows, width),
        ],
        in_specs=[VMEM, ANYWHERE, ANYWHERE],
        out_specs=[VMEM] * 3,
        scratch_shapes=[
            pltpu.VMEM((rows, width), LOW),
            pltpu.VMEM((rows, inner), LOW),
            pltpu.VMEM((width, inner), LOW),
            pltpu.VMEM((inner, width), LOW),
            pltpu.SemaphoreType.DMA((2, steps)),
        ],
        compiler_params=pltpu.CompilerParams(vmem_limit_bytes=60 * MIB),
        name="expert",
    )(arrived, first_weight, second_weight)
    back = exchange(send)
    grad_second = dot(hidden, grads, ((0,), (0,))).astype(LOW)

    send, grad_low, slot_out, grad_slot_in = pl.pallas_call(
        logit_kernel,
        out_shape=[
            shaped(LOW, *pair_shape),
            shaped(LOW, length, slots),
            shaped(LOW, slots, width),
            shaped(LOW, slots, width),
        ],
        in_specs=[VMEM] * 5,
        out_specs=[VMEM] * 4,
        compiler_params=pltpu.CompilerParams(vmem_limit_bytes=32 * MIB),
        name="logit",
    )(back, tokens, cotangent, dispatch, combine)
    terms = exchange(send)
    mixed_out = dot(combine.astype(LOW), slot_out, ((1,), (0,))).astype(LOW)
    through_slots = dot(dispatch.astype(LOW), grad_slot_in, ((1,), (0,)))
    through_keys = dot(grad_low, keys_all, ((1,), (0,)))
    grad_tokens = (through_slots + through_keys).astype(LOW)
    grad_keys = pl.pallas_call(
        sum_kernel,
        out_shape=shaped(jnp.float32, SLOTS_EXP, width),
        in_specs=[VMEM],
        out_specs=VMEM,
        compiler_params=pltpu.CompilerParams(vmem_limit_bytes=16 * MIB),
        name="total",
    )(terms)
    return (mixed_out[None], grad_tokens[None], grad_keys, grad_second[None])


def solution(mesh):
    in_specs = (
        P(AXES, None, None),
        P(AXES, None),
        P(AXES, None, None),
        P(AXES, None, None),
        P(AXES, None, None),
    )
    out_specs = (
        P(AXES, None, None),
        P(AXES, None, None),
        P(AXES, None),
        P(AXES, None, None),
    )
    return jax.shard_map(local, mesh=mesh, in_specs=in_specs, out_specs=out_specs, check_vma=False)
```

time: 140 us -> 117 us (0.84)
  blocking collectives: 52.1 us -> 78.4 us
  matrix products: 31.5 us -> 8.9 us
  waiting for transfers between devices: 27.2 us -> 6 us
  Pallas kernels: 0 us -> 17 us
  local copies, waits for them, and re-layouts: 13.6 us -> 1.14 us
  other arithmetic: 5.34 us -> 0 us
  starting transfers between devices: 8.61 us -> 4.31 us
    all_to_all x2 -> x3, blocking collectives: 52.1 us -> 78.4 us  [exchange(): return lax.all_to_all(blocks, AXES, split_axis=0, concat_axis=0, tiled=True)]
    dot_general x13 -> x4, matrix products: 31.5 us -> 8.9 us  [dot(): lax.dot_general(a, b, (dims, ((), ())), preferred_element_type=jnp.float32)]
    all_to_all x2 -> x1, waiting for transfers between devices: 27.2 us -> 6 us  [exchange(): return lax.all_to_all(blocks, AXES, split_axis=0, concat_axis=0, tiled=True)]
    pallas_call x0 -> x4, Pallas kernels: none -> 17 us  [the longest x1 12.8 us: local(): pl.pallas_call(expert_kernel, out_shape=[shaped(LOW, *twin_shape), shaped...]
    reshape x10 -> x0, local copies, waits for them, and re-layouts: 7.7 us -> none  [the longest x1 2.07 us: local(): grad_slot_in = back[:, SLOTS_EXP:].reshape(slots, width)]
    all_to_all x2 -> x1, starting transfers between devices: 8.61 us -> 4.31 us  [exchange(): return lax.all_to_all(blocks, AXES, split_axis=0, concat_axis=0, tiled=True)]
    concatenate x2 -> x0, other arithmetic: 3.79 us -> none  [the longest x1 2.44 us: local(): jnp.concatenate([expert_out.reshape(parts), grad_rows_in.reshape(parts)],...]
    slice x2 -> x0, local copies, waits for them, and re-layouts: 2.65 us -> none  [the longest x1 1.74 us: local(): grad_slot_in = back[:, SLOTS_EXP:].reshape(slots, width)]
  transfers between devices with their start and end apart: 2 -> 1, of which waited for: 2 -> 1; matrix products, arithmetic and copies ran while one was open for 7% -> 8% of each run, Pallas kernels for 0% -> 0%
where the time goes in v2:
time: 117 us; the launch traced here: 116 us
  blocking collectives  78.4 us (67%)
  Pallas kernels  17 us (15%)
  matrix products  8.9 us (8%)
  waiting for transfers between devices  6 us (5%)
  starting transfers between devices  4.31 us (4%)
    all_to_all x3, blocking collectives, exchange(): return lax.all_to_all(blocks, AXES, split_axis=0, concat_axis=0, tiled=True)  78.4 us
    pallas_call x1, Pallas kernels, local(): pl.pallas_call(expert_kernel, out_shape=[shaped(LOW, *twin_shape), shaped...  12.8 us
    dot_general x4, matrix products, dot(): lax.dot_general(a, b, (dims, ((), ())), preferred_element_type=jnp.float32)  8.9 us
    all_to_all x1, waiting for transfers between devices, exchange(): return lax.all_to_all(blocks, AXES, split_axis=0, concat_axis=0, tiled=True)  6 us
    all_to_all x1, starting transfers between devices, exchange(): return lax.all_to_all(blocks, AXES, split_axis=0, concat_axis=0, tiled=True)  4.31 us
  transfers between devices with their start and end apart: 1, of which 1 were waited for; matrix products, arithmetic and copies ran while one was open for 8% of the time, Pallas kernels for 0%

profile of v2, /device:TPU:1, one launch (start us, length us, event | category | flops | bytes accessed | tf_op | source)
XLA Modules:
  0.0 116.5 jit_solution(1977921375120124383)
XLA Ops:
  0.6 0.0 copy-start.1
  0.6 0.0 copy-start
  0.7 1.1 broadcast_in_dim.15
  1.8 26.2 %all_to_all.20.keys = bf16[128,2,1280]{2,1,0:T(2,128)(2,1)S(1)} all-to-all(bf16[128,2,1280]{2,1,0:T(2,128)(2,1)S(1)} %broadcast_in_dim.15), channel_id=1, replica_groups=mesh['dp'=8,'mp'=16] {'dp','mp'}, dimensions={0} | all-to-all | bytes 1310720 | tf_op jit(solution)/shard_map/all_to_all | solution.py:30
  28.0 0.0 copy-done.1
  28.0 0.0 copy-done
  28.0 1.3 %route.1 = (bf16[128,2,2,1280]{3,2,1,0:T(2,128)(2,1)S(1)}, f32[256,256]{1,0:T(8,128)S(1)}, f32[256,256]{1,0:T(8,128)S(1)}, bf16[256,1280]{1,0:T(8,128)(2,1)S(1)}) custom-call(bf16[256,1280]{1,0:T(8,128)(2,1)S(1)} %bitcast.16, bf16[256,1280]{1,0:T(8,128)(2,1)S(1)} %bitcast.18, bf16[128,2,1280]{2,1,0:T(2,128)(2,1)S(1)} %all_to_all.20.keys), custom_call_target="tpu_custom_call" | custom-call | tf_op jit(solution)/shard_map/route/pallas_call | solution.py:141
  29.3 26.0 %all_to_all.21.arrived = bf16[128,2,2,1280]{3,2,1,0:T(2,128)(2,1)} all-to-all(bf16[128,2,2,1280]{3,2,1,0:T(2,128)(2,1)S(1)} %get-tuple-element.16), channel_id=1, replica_groups=mesh['dp'=8,'mp'=16] {'dp','mp'}, dimensions={0} | all-to-all | bytes 2621440 | tf_op jit(solution)/shard_map/all_to_all | solution.py:30
  55.3 12.8 %expert.1 = (bf16[128,2,2,1280]{3,2,1,0:T(2,128)(2,1)}, bf16[256,2560]{1,0:T(8,128)(2,1)}, bf16[256,1280]{1,0:T(8,128)(2,1)}) custom-call(bf16[128,2,2,1280]{3,2,1,0:T(2,128)(2,1)} %all_to_all.21.arrived, bf16[1280,2560]{1,0:T(8,128)(2,1)} %bitcast.20, bf16[2560,1280]{1,0:T(8,128)(2,1)} %bitcast.21), custom_call_target="tpu_custom_call" | custom-call | tf_op jit(solution)/shard_map/expert/pallas_call | solution.py:158
  68.2 26.2 %all_to_all.22.back = bf16[128,2,2,1280]{3,2,1,0:T(2,128)(2,1)S(1)} all-to-all(bf16[128,2,2,1280]{3,2,1,0:T(2,128)(2,1)} %get-tuple-element.17), channel_id=1, replica_groups=mesh['dp'=8,'mp'=16] {'dp','mp'}, dimensions={0} | all-to-all | bytes 2621440 | tf_op jit(solution)/shard_map/all_to_all | solution.py:30
  94.4 2.0 %logit.1 = (bf16[128,2,1280]{2,1,0:T(2,128)(2,1)}, bf16[256,256]{1,0:T(8,128)(2,1)S(1)}, bf16[256,1280]{1,0:T(8,128)(2,1)S(1)}, bf16[256,1280]{1,0:T(8,128)(2,1)S(1)}) custom-call(bf16[128,2,2,1280]{3,2,1,0:T(2,128)(2,1)S(1)} %all_to_all.22.back, bf16[256,1280]{1,0:T(8,128)(2,1)S(1)} %bitcast.17, bf16[256,1280]{1,0:T(8,128)(2,1)S(1)} %bitcast.19, ...), custom_call_target="tpu_custom_call" | custom-call | tf_op jit(solution)/shard_map/logit/pallas_call | solution.py:180
  96.3 4.3 %all-to-all-start.3 = ((bf16[128,2,1280]{2,1,0:T(2,128)(2,1)}), bf16[128,2,1280]{2,1,0:T(2,128)(2,1)S(1)}, u32[]{:S(2)}, u32[]{:S(2)}) async-start(bf16[128,2,1280]{2,1,0:T(2,128)(2,1)} %get-tuple-element.23), calls=%async_computation.3 | async-start | bytes 1310720 | tf_op jit(solution)/shard_map/all_to_all | solution.py:30
  100.6 6.2 %fusion = bf16[1,2560,1280]{2,1,0:T(8,128)(2,1)} fusion(bf16[256,2560]{1,0:T(8,128)(2,1)} %get-tuple-element.24, bf16[256,1280]{1,0:T(8,128)(2,1)} %get-tuple-element.25), kind=kOutput, calls=%fused_computation.1 | convolution fusion | flops 1680998400 | bytes 8519680 | tf_op jit(solution)/shard_map/dot_general | solution.py:34
  106.8 1.2 %fusion.2 = bf16[1,256,1280]{2,1,0:T(8,128)(2,1)} fusion(bf16[256,1280]{1,0:T(8,128)(2,1)S(1)} %get-tuple-element.19, f32[256,256]{1,0:T(8,128)S(1)} %get-tuple-element.15.combine_in), kind=kOutput, calls=%fused_computation.5 | convolution fusion | flops 168165376 | bytes 1572864 | tf_op jit(solution)/shard_map/dot_general | solution.py:34
  108.0 0.3 fusion.4
  108.4 1.2 %fusion.3 = bf16[1,256,1280]{2,1,0:T(8,128)(2,1)} fusion(f32[256,1280]{1,0:T(8,128)S(1)} %fusion.4, bf16[256,256]{1,0:T(8,128)(2,1)S(1)} %get-tuple-element.21, bf16[256,1280]{1,0:T(8,128)(2,1)S(1)} %get-tuple-element.22), kind=kOutput, calls=%fused_computation.6 | convolution fusion | flops 168427520 | bytes 2752512 | tf_op jit(solution)/shard_map/dot_general | solution.py:34
  109.5 6.0 %all-to-all-done.3.terms = bf16[128,2,1280]{2,1,0:T(2,128)(2,1)S(1)} async-done(((bf16[128,2,1280]{2,1,0:T(2,128)(2,1)}), bf16[128,2,1280]{2,1,0:T(2,128)(2,1)S(1)}, u32[]{:S(2)}, u32[]{:S(2)}) %all-to-all-start.3) | async-done | bytes 655392 | tf_op jit(solution)/shard_map/all_to_all | solution.py:30
  115.5 0.9 total.1
Async XLA Ops:
  0.6 27.4 %copy-start.1 = (bf16[1,256,1280]{2,1,0:T(8,128)(2,1)S(1)}, bf16[1,256,1280]{2,1,0:T(8,128)(2,1)}, u32[]{:S(2)}) copy-start(bf16[1,256,1280]{2,1,0:T(8,128)(2,1)} %param.9) | copy-start | bytes 1966084
  0.6 27.4 %copy-start = (bf16[1,256,1280]{2,1,0:T(8,128)(2,1)S(1)}, bf16[1,256,1280]{2,1,0:T(8,128)(2,1)}, u32[]{:S(2)}) copy-start(bf16[1,256,1280]{2,1,0:T(8,128)(2,1)} %param.5) | copy-start | bytes 1966084
  96.3 19.2 %all-to-all-start.3 = ((bf16[128,2,1280]{2,1,0:T(2,128)(2,1)}), bf16[128,2,1280]{2,1,0:T(2,128)(2,1)S(1)}, u32[]{:S(2)}, u32[]{:S(2)}) async-start(bf16[128,2,1280]{2,1,0:T(2,128)(2,1)} %get-tuple-element.23), calls=%async_computation.3 | async-start | bytes 1310720 | tf_op jit(solution)/shard_map/all_to_all | solution.py:30

commit v3 on v2

v3 whole, which is shorter than its diff:
```python
import jax
import jax.numpy as jnp
from jax import lax
from jax.experimental import pallas as pl
from jax.experimental.pallas import tpu as pltpu
from jax.sharding import PartitionSpec as P

SLOTS_EXP = 2
AXES = ("dp", "mp")
LOW = jnp.bfloat16
FF_BLOCK = 512
D_BLOCK = 256
SEND_PARTS = 4
MIB = 1 << 20

inv_root_two = 0.7071067811865476
inv_root_tau = 0.3989422804014327


def gelu_pair(values):
    cumulative = 0.5 * (1.0 + lax.erf(values * inv_root_two))
    density = jnp.exp(-0.5 * values * values) * inv_root_tau
    return (values * cumulative, cumulative + values * density)


def device_count():
    return lax.axis_size(AXES)


def exchange(blocks):
    return lax.all_to_all(blocks, AXES, split_axis=0, concat_axis=0, tiled=True)


def dot(a, b, dims):
    return lax.dot_general(a, b, (dims, ((), ())), preferred_element_type=jnp.float32)


def softmax(values, axis):
    powers = jnp.exp(values - jnp.max(values, axis=axis, keepdims=True))
    return powers / jnp.sum(powers, axis=axis, keepdims=True)


def route_kernel(
    tokens, cotangent, keys, send, dispatch_out, combine_out, keys_hbm, keys_flat, sem
):
    pairs = keys.shape[0]
    slots, width = keys_flat.shape
    keys_flat[...] = keys[...].reshape(slots, width)
    keep = pltpu.make_async_copy(keys_flat, keys_hbm, sem)
    keep.start()
    logits = dot(tokens[...], keys_flat[...], ((1,), (1,)))
    dispatch = softmax(logits, 0)
    dispatch_out[...] = dispatch
    slots_in = dot(dispatch.astype(LOW), tokens[...], ((0,), (0,))).astype(LOW)
    send[:, 0] = slots_in.reshape(pairs, SLOTS_EXP, width)
    combine = softmax(logits, 1)
    combine_out[...] = combine
    grad_slot_out = dot(combine.astype(LOW), cotangent[...], ((0,), (0,))).astype(LOW)
    send[:, 1] = grad_slot_out.reshape(pairs, SLOTS_EXP, width)
    keep.wait()


def expert_kernel(arrived, first, second, send, hidden, grads, rows, grad_pre):
    width, inner = first.shape
    pairs = arrived.shape[0]
    rows[...] = arrived[:, 0].reshape(rows.shape)
    grads[...] = arrived[:, 1].reshape(rows.shape)
    for i in range(inner // FF_BLOCK):
        block = pl.ds(i * FF_BLOCK, FF_BLOCK)
        pre_act = dot(rows[...], first[:, block], ((1,), (0,)))
        grad_hidden = dot(grads[...], second[block, :], ((1,), (1,)))
        active, slope = gelu_pair(pre_act)
        hidden[:, block] = active.astype(LOW)
        grad_pre[:, block] = (grad_hidden * slope).astype(LOW)
    for j in range(width // D_BLOCK):
        block = pl.ds(j * D_BLOCK, D_BLOCK)
        out = dot(hidden[...], second[:, block], ((1,), (0,))).astype(LOW)
        send[:, 0, :, block] = out.reshape(pairs, SLOTS_EXP, D_BLOCK)
        back = dot(grad_pre[...], first[block, :], ((1,), (1,))).astype(LOW)
        send[:, 1, :, block] = back.reshape(pairs, SLOTS_EXP, D_BLOCK)


def logit_kernel(
    back,
    tokens,
    cotangent,
    dispatch_in,
    combine_in,
    send_hbm,
    grad_low_out,
    send,
    slot_out,
    grad_slot_in,
    sems,
):
    pairs, each, width = send.shape
    slot_out[...] = back[:, 0].reshape(slot_out.shape)
    grad_slot_in[...] = back[:, 1].reshape(slot_out.shape)
    dispatch = dispatch_in[...]
    combine = combine_in[...]
    grad_combine = dot(cotangent[...], slot_out[...], ((1,), (1,)))
    grad_dispatch = dot(tokens[...], grad_slot_in[...], ((1,), (1,)))
    grad_logits = dispatch * (
        grad_dispatch - jnp.sum(dispatch * grad_dispatch, axis=0, keepdims=True)
    ) + combine * (grad_combine - jnp.sum(combine * grad_combine, axis=1, keepdims=True))
    grad_low = grad_logits.astype(LOW)
    grad_low_out[...] = grad_low
    terms = dot(grad_low, tokens[...], ((0,), (0,))).astype(LOW)
    some = pairs // SEND_PARTS
    copies = []
    for j in range(SEND_PARTS):
        part = pl.ds(j * some, some)
        send[part] = terms[j * some * each : (j + 1) * some * each].reshape(some, each, width)
        copies.append(
            pltpu.make_async_copy(send.at[part], send_hbm.at[part], sems.at[j])
        )
        copies[-1].start()
    for copy in copies:
        copy.wait()


def finish_kernel(
    back, dispatch, combine, grad_low, keys, mixed_out, grad_tokens, slot_out, grad_slot_in
):
    slot_out[...] = back[:, 0].reshape(slot_out.shape)
    mixed_out[...] = dot(combine[...].astype(LOW), slot_out[...], ((1,), (0,))).astype(LOW)
    grad_slot_in[...] = back[:, 1].reshape(slot_out.shape)
    through_slots = dot(dispatch[...].astype(LOW), grad_slot_in[...], ((1,), (0,)))
    through_keys = dot(grad_low[...], keys[...], ((1,), (0,)))
    grad_tokens[...] = (through_slots + through_keys).astype(LOW)


def sum_kernel(terms, total):
    pairs, each, width = terms.shape
    owner = lax.broadcasted_iota(jnp.int32, (8, pairs * each), 0)
    slot = lax.broadcasted_iota(jnp.int32, (8, pairs * each), 1) % each
    chosen = jnp.where(owner == slot, 1.0, 0.0).astype(LOW)
    flat = terms[...].reshape(pairs * each, width)
    total[...] = dot(chosen, flat, ((1,), (0,)))[0:each]


def spread_kernel(keys, send):
    send[...] = jnp.broadcast_to(keys[...][None], send.shape)


BESIDE = pl.CostEstimate(flops=20_000_000_000, bytes_accessed=1_000_000, transcendentals=0)
VMEM = pl.BlockSpec(memory_space=pltpu.VMEM)
HBM = pl.BlockSpec(memory_space=pltpu.HBM)


def in_hbm(dtype, *shape):
    return pltpu.HBM(shape, dtype)


def shaped(dtype, *shape):
    return jax.ShapeDtypeStruct(shape, dtype)


def local(tokens, slot_keys, weight_in, weight_out, cotangent):
    devices = device_count()
    length, width = tokens.shape[1:]
    inner = weight_in.shape[2]
    slots = devices * SLOTS_EXP
    tokens, cotangent = tokens[0], cotangent[0]
    first_weight, second_weight = weight_in[0], weight_out[0]
    pair_shape = (devices, SLOTS_EXP, width)
    twin_shape = (devices, 2, SLOTS_EXP, width)
    send = pl.pallas_call(
        spread_kernel,
        out_shape=shaped(LOW, *pair_shape),
        in_specs=[VMEM],
        out_specs=VMEM,
        cost_estimate=BESIDE,
        compiler_params=pltpu.CompilerParams(vmem_limit_bytes=4 * MIB),
        name="spread",
    )(slot_keys)
    keys = exchange(send)

    send, dispatch, combine, keys_all = pl.pallas_call(
        route_kernel,
        out_shape=[
            shaped(LOW, *twin_shape),
            shaped(jnp.float32, length, slots),
            shaped(jnp.float32, length, slots),
            in_hbm(LOW, slots, width),
        ],
        in_specs=[VMEM] * 3,
        out_specs=[VMEM] * 3 + [HBM],
        scratch_shapes=[pltpu.VMEM((slots, width), LOW), pltpu.SemaphoreType.DMA],
        cost_estimate=BESIDE,
        compiler_params=pltpu.CompilerParams(vmem_limit_bytes=8 * MIB),
        name="route",
    )(tokens, cotangent, keys)
    arrived = exchange(send)

    rows = arrived.shape[0] * SLOTS_EXP
    send, hidden, grads = pl.pallas_call(
        expert_kernel,
        out_shape=[
            shaped(LOW, *twin_shape),
            shaped(LOW, rows, inner),
            shaped(LOW, rows, width),
        ],
        in_specs=[VMEM] * 3,
        out_specs=[VMEM] * 3,
        scratch_shapes=[
            pltpu.VMEM((rows, width), LOW),
            pltpu.VMEM((rows, inner), LOW),
        ],
        compiler_params=pltpu.CompilerParams(vmem_limit_bytes=10 * MIB),
        name="expert",
    )(arrived, first_weight, second_weight)
    back = exchange(send)
    grad_second = dot(hidden, grads, ((0,), (0,))).astype(LOW)

    send, grad_low = pl.pallas_call(
        logit_kernel,
        out_shape=[in_hbm(LOW, *pair_shape), shaped(LOW, length, slots)],
        in_specs=[VMEM] * 5,
        out_specs=[HBM, VMEM],
        scratch_shapes=[
            pltpu.VMEM(pair_shape, LOW),
            pltpu.VMEM((slots, width), LOW),
            pltpu.VMEM((slots, width), LOW),
            pltpu.SemaphoreType.DMA((SEND_PARTS,)),
        ],
        compiler_params=pltpu.CompilerParams(vmem_limit_bytes=8 * MIB),
        name="logit",
    )(back, tokens, cotangent, dispatch, combine)
    terms = exchange(send)
    mixed_out, grad_tokens = pl.pallas_call(
        finish_kernel,
        out_shape=[shaped(LOW, length, width)] * 2,
        in_specs=[VMEM] * 5,
        out_specs=[VMEM] * 2,
        scratch_shapes=[pltpu.VMEM((slots, width), LOW)] * 2,
        compiler_params=pltpu.CompilerParams(vmem_limit_bytes=8 * MIB),
        name="finish",
    )(back, dispatch, combine, grad_low, keys_all)
    grad_keys = pl.pallas_call(
        sum_kernel,
        out_shape=shaped(jnp.float32, SLOTS_EXP, width),
        in_specs=[VMEM],
        out_specs=VMEM,
        compiler_params=pltpu.CompilerParams(vmem_limit_bytes=4 * MIB),
        name="total",
    )(terms)
    return (mixed_out[None], grad_tokens[None], grad_keys, grad_second[None])


def solution(mesh):
    in_specs = (
        P(AXES, None, None),
        P(AXES, None),
        P(AXES, None, None),
        P(AXES, None, None),
        P(AXES, None, None),
    )
    out_specs = (
        P(AXES, None, None),
        P(AXES, None, None),
        P(AXES, None),
        P(AXES, None, None),
    )
    return jax.shard_map(local, mesh=mesh, in_specs=in_specs, out_specs=out_specs, check_vma=False)
```

time: 117 us -> 111 us (0.949)
  Pallas kernels: 17 us -> 12.9 us
  matrix products: 8.9 us -> 5.88 us
  waiting for transfers between devices: 6 us -> 7.38 us
    pallas_call x1, Pallas kernels: 12.8 us -> 7.13 us  [local(): pl.pallas_call(expert_kernel, out_shape=[shaped(LOW, *twin_shape), shaped...]
    dot_general x4 -> x1, matrix products: 8.9 us -> 5.88 us  [dot(): lax.dot_general(a, b, (dims, ((), ())), preferred_element_type=jnp.float32)]
    pallas_call x1 -> x3, Pallas kernels: 1.95 us -> 3.59 us  [the longest x1 1.92 us: local(): pl.pallas_call(logit_kernel, out_shape=[in_hbm(LOW, *pair_shape), shaped(...]
    all_to_all x1, waiting for transfers between devices: 6 us -> 7.38 us  [exchange(): return lax.all_to_all(blocks, AXES, split_axis=0, concat_axis=0, tiled=True)]
    unnamed x4 -> x26, local copies, waits for them, and re-layouts: 0.01 us -> 1.38 us
  transfers between devices with their start and end apart: 1 -> 1, of which waited for: 1 -> 1; matrix products, arithmetic and copies ran while one was open for 8% -> 5% of each run, Pallas kernels for 0% -> 1%
where the time goes in v3:
time: 111 us
  blocking collectives  78.1 us (70%)
  Pallas kernels  12.9 us (12%)
  waiting for transfers between devices  7.38 us (7%)
  matrix products  5.88 us (5%)
  starting transfers between devices  4.31 us (4%)
  local copies, waits for them, and re-layouts  1.38 us (1%)
    all_to_all x3, blocking collectives, exchange(): return lax.all_to_all(blocks, AXES, split_axis=0, concat_axis=0, tiled=True)  78.1 us
    all_to_all x1, waiting for transfers between devices, exchange(): return lax.all_to_all(blocks, AXES, split_axis=0, concat_axis=0, tiled=True)  7.38 us
    pallas_call x1, Pallas kernels, local(): pl.pallas_call(expert_kernel, out_shape=[shaped(LOW, *twin_shape), shaped...  7.13 us
    dot_general x1, matrix products, dot(): lax.dot_general(a, b, (dims, ((), ())), preferred_element_type=jnp.float32)  5.88 us
    all_to_all x1, starting transfers between devices, exchange(): return lax.all_to_all(blocks, AXES, split_axis=0, concat_axis=0, tiled=True)  4.31 us
  transfers between devices with their start and end apart: 1, of which 1 were waited for; matrix products, arithmetic and copies ran while one was open for 5% of the time, Pallas kernels for 1%

profile of v3, /device:TPU:1, one launch (start us, length us, event | category | flops | bytes accessed | tf_op | source)
XLA Modules:
  0.0 110.7 jit_solution(367372455181719980)
XLA Ops:
  0.6 0.0 copy-start.8
  0.6 0.7 copy-done.8
  1.3 0.1 spread.1
  1.4 0.0 copy-start.4
  1.4 0.0 copy-start.5
  1.4 26.2 %all_to_all.20.keys = bf16[128,2,1280]{2,1,0:T(2,128)(2,1)S(1)} all-to-all(bf16[128,2,1280]{2,1,0:T(2,128)(2,1)S(1)} %spread.1), channel_id=1, replica_groups=mesh['dp'=8,'mp'=16] {'dp','mp'}, dimensions={0} | all-to-all | bytes 1310720 | tf_op jit(solution)/shard_map/all_to_all | solution.py:31
  27.6 0.0 slice-start
  27.6 0.0 slice-start.2
  27.6 0.0 copy-done.4
  27.6 0.0 copy-done.5
  27.6 0.0 slice-start.1
  27.7 0.0 slice-start.3
  27.7 1.3 %route.1 = (bf16[128,2,2,1280]{3,2,1,0:T(2,128)(2,1)S(1)}, f32[256,256]{1,0:T(8,128)S(1)}, f32[256,256]{1,0:T(8,128)S(1)}, bf16[256,1280]{1,0:T(8,128)(2,1)}) custom-call(bf16[256,1280]{1,0:T(8,128)(2,1)S(1)} %bitcast.16, bf16[256,1280]{1,0:T(8,128)(2,1)S(1)} %bitcast.18, bf16[128,2,1280]{2,1,0:T(2,128)(2,1)S(1)} %all_to_all.20.keys), custom_call_target="tpu_custom_call" | custom-call | flops 20000000000 | bytes 1000000 | tf_op jit(solution)/shard_map/route/pallas_call | solution.py:179
  29.0 0.0 copy-start
  29.0 25.9 %all_to_all.21.arrived = bf16[128,2,2,1280]{3,2,1,0:T(2,128)(2,1)S(1)} all-to-all(bf16[128,2,2,1280]{3,2,1,0:T(2,128)(2,1)S(1)} %get-tuple-element.15), channel_id=1, replica_groups=mesh['dp'=8,'mp'=16] {'dp','mp'}, dimensions={0} | all-to-all | bytes 2621440 | tf_op jit(solution)/shard_map/all_to_all | solution.py:31
  54.9 0.0 slice-done
  54.9 0.0 slice-done.2
  54.9 0.0 slice-done.1
  54.9 0.0 slice-done.3
  55.0 7.1 %expert.1 = (bf16[128,2,2,1280]{3,2,1,0:T(2,128)(2,1)S(1)}, bf16[256,2560]{1,0:T(8,128)(2,1)S(1)}, bf16[256,1280]{1,0:T(8,128)(2,1)S(1)}) custom-call(bf16[128,2,2,1280]{3,2,1,0:T(2,128)(2,1)S(1)} %all_to_all.21.arrived, bf16[1280,2560]{1,0:T(8,128)(2,1)S(1)} %bitcast.12, bf16[2560,1280]{1,0:T(8,128)(2,1)S(1)} %bitcast.15), custom_call_target="tpu_custom_call" | custom-call | tf_op jit(solution)/shard_map/expert/pallas_call | solution.py:197
  62.1 0.0 copy-start.2
  62.1 26.0 %all_to_all.22.back = bf16[128,2,2,1280]{3,2,1,0:T(2,128)(2,1)S(1)} all-to-all(bf16[128,2,2,1280]{3,2,1,0:T(2,128)(2,1)S(1)} %get-tuple-element.16), channel_id=1, replica_groups=mesh['dp'=8,'mp'=16] {'dp','mp'}, dimensions={0} | all-to-all | bytes 2621440 | tf_op jit(solution)/shard_map/all_to_all | solution.py:31
  88.1 0.0 copy-done.2
  88.1 0.0 copy-done
  88.1 1.9 %logit.1 = (bf16[128,2,1280]{2,1,0:T(2,128)(2,1)}, bf16[256,256]{1,0:T(8,128)(2,1)S(1)}) custom-call(bf16[128,2,2,1280]{3,2,1,0:T(2,128)(2,1)S(1)} %all_to_all.22.back, bf16[256,1280]{1,0:T(8,128)(2,1)S(1)} %bitcast.17, bf16[256,1280]{1,0:T(8,128)(2,1)S(1)} %bitcast.19, f32[256,256]{1,0:T(8,128)S(1)} %get-tuple-element.17.dispatch_in.dispatch, ...), custom_call_target="tpu_custom_call" | custom-call | tf_op jit(solution)/shard_map/logit/pallas_call | solution.py:216
  90.0 0.0 copy-start.6
  90.0 0.6 copy-done.6
  90.7 4.3 %all-to-all-start.3 = ((bf16[128,2,1280]{2,1,0:T(2,128)(2,1)}), bf16[128,2,1280]{2,1,0:T(2,128)(2,1)S(1)}, u32[]{:S(2)}, u32[]{:S(2)}) async-start(bf16[128,2,1280]{2,1,0:T(2,128)(2,1)} %get-tuple-element.23), calls=%async_computation.3 | async-start | bytes 1310720 | tf_op jit(solution)/shard_map/all_to_all | solution.py:31
  95.0 0.0 copy-start.1
  95.0 0.0 copy-start.3
  95.0 0.0 copy-start.7
  95.0 5.9 %fusion = bf16[1,2560,1280]{2,1,0:T(8,128)(2,1)} fusion(bf16[256,2560]{1,0:T(8,128)(2,1)S(1)} %get-tuple-element.24, bf16[256,1280]{1,0:T(8,128)(2,1)} %copy-done.2), kind=kOutput, calls=%fused_computation.1 | convolution fusion | flops 1680998400 | bytes 8519680 | tf_op jit(solution)/shard_map/dot_general | solution.py:35
  100.9 0.0 copy-done.1
  100.9 0.0 copy-done.3
  100.9 0.0 copy-done.7
  100.9 1.6 %finish.1 = (bf16[256,1280]{1,0:T(8,128)(2,1)}, bf16[256,1280]{1,0:T(8,128)(2,1)}) custom-call(bf16[128,2,2,1280]{3,2,1,0:T(2,128)(2,1)S(1)} %all_to_all.22.back, f32[256,256]{1,0:T(8,128)S(1)} %get-tuple-element.17.dispatch_in.dispatch, f32[256,256]{1,0:T(8,128)S(1)} %copy-done.1, bf16[256,256]{1,0:T(8,128)(2,1)S(1)} %copy-done.7, ...), custom_call_target="tpu_custom_call" | custom-call | tf_op jit(solution)/shard_map/finish/pallas_call | solution.py:231
  102.5 7.4 %all-to-all-done.3.terms = bf16[128,2,1280]{2,1,0:T(2,128)(2,1)S(1)} async-done(((bf16[128,2,1280]{2,1,0:T(2,128)(2,1)}), bf16[128,2,1280]{2,1,0:T(2,128)(2,1)S(1)}, u32[]{:S(2)}, u32[]{:S(2)}) %all-to-all-start.3) | async-done | bytes 655392 | tf_op jit(solution)/shard_map/all_to_all | solution.py:31
  109.9 0.8 total.1
  (2 shorter events, 0.0 us)
Async XLA Ops:
  0.6 0.7 copy-start.8
  1.4 26.2 %copy-start.4 = (bf16[1,256,1280]{2,1,0:T(8,128)(2,1)S(1)}, bf16[1,256,1280]{2,1,0:T(8,128)(2,1)}, u32[]{:S(2)}) copy-start(bf16[1,256,1280]{2,1,0:T(8,128)(2,1)} %param.5) | copy-start | bytes 1966084
  1.4 26.2 %copy-start.5 = (bf16[1,256,1280]{2,1,0:T(8,128)(2,1)S(1)}, bf16[1,256,1280]{2,1,0:T(8,128)(2,1)}, u32[]{:S(2)}) copy-start(bf16[1,256,1280]{2,1,0:T(8,128)(2,1)} %param.9) | copy-start | bytes 1966084
  27.6 27.3 %slice-start = ((s8[6553600]{0:T(1024)(128)(4,1)}), s8[4194304]{0:T(1024)(128)(4,1)S(1)}, s32[]{:S(2)}) async-start(s8[6553600]{0:T(1024)(128)(4,1)} %bitcast.10), calls=%async_computation.4 | async-start | bytes 8388608
  27.6 27.3 %slice-start.2 = ((s8[6553600]{0:T(1024)(128)(4,1)}), s8[4194304]{0:T(1024)(128)(4,1)S(1)}, s32[]{:S(2)}) async-start(s8[6553600]{0:T(1024)(128)(4,1)} %bitcast.13), calls=%async_computation.6 | async-start | bytes 8388608
  27.6 27.3 %slice-start.1 = ((s8[6553600]{0:T(1024)(128)(4,1)}), s8[2359296]{0:T(1024)(128)(4,1)S(1)}, s32[]{:S(2)}) async-start(s8[6553600]{0:T(1024)(128)(4,1)} %bitcast.10), calls=%async_computation.5 | async-start | bytes 4718592
  27.7 27.3 %slice-start.3 = ((s8[6553600]{0:T(1024)(128)(4,1)}), s8[2359296]{0:T(1024)(128)(4,1)S(1)}, s32[]{:S(2)}) async-start(s8[6553600]{0:T(1024)(128)(4,1)} %bitcast.13), calls=%async_computation.7 | async-start | bytes 4718592
  29.0 59.1 %copy-start = (f32[256,256]{1,0:T(8,128)}, f32[256,256]{1,0:T(8,128)S(1)}, u32[]{:S(2)}) copy-start(f32[256,256]{1,0:T(8,128)S(1)} %get-tuple-element.18.combine_in.combine) | copy-start | bytes 786436
  62.1 26.0 %copy-start.2 = (bf16[256,1280]{1,0:T(8,128)(2,1)}, bf16[256,1280]{1,0:T(8,128)(2,1)S(1)}, u32[]{:S(2)}) copy-start(bf16[256,1280]{1,0:T(8,128)(2,1)S(1)} %get-tuple-element.25) | copy-start | bytes 1966084
  90.0 0.7 copy-start.6
  90.7 19.2 %all-to-all-start.3 = ((bf16[128,2,1280]{2,1,0:T(2,128)(2,1)}), bf16[128,2,1280]{2,1,0:T(2,128)(2,1)S(1)}, u32[]{:S(2)}, u32[]{:S(2)}) async-start(bf16[128,2,1280]{2,1,0:T(2,128)(2,1)} %get-tuple-element.23), calls=%async_computation.3 | async-start | bytes 1310720 | tf_op jit(solution)/shard_map/all_to_all | solution.py:31
  95.0 5.9 %copy-start.1 = (f32[256,256]{1,0:T(8,128)S(1)}, f32[256,256]{1,0:T(8,128)}, u32[]{:S(2)}) copy-start(f32[256,256]{1,0:T(8,128)} %copy-done) | copy-start | bytes 786436
  95.0 5.9 %copy-start.3 = (bf16[256,1280]{1,0:T(8,128)(2,1)S(1)}, bf16[256,1280]{1,0:T(8,128)(2,1)}, u32[]{:S(2)}) copy-start(bf16[256,1280]{1,0:T(8,128)(2,1)} %get-tuple-element.20.keys) | copy-start | bytes 1966084
  95.0 5.9 %copy-start.7 = (bf16[256,256]{1,0:T(8,128)(2,1)S(1)}, bf16[256,256]{1,0:T(8,128)(2,1)}, u32[]{:S(2)}) copy-start(bf16[256,256]{1,0:T(8,128)(2,1)} %copy-done.6) | copy-start | bytes 393220

commit v4 on v3

--- a/solution.py
+++ b/solution.py
@@ -3,14 +3,17 @@
 from jax import lax
 from jax.experimental import pallas as pl
 from jax.experimental.pallas import tpu as pltpu
+from jax.sharding import Mesh
 from jax.sharding import PartitionSpec as P
 
 SLOTS_EXP = 2
-AXES = ("dp", "mp")
+ACROSS = ("dp", "chip")
+AXES = ("dp", "chip", "core")
+CORES = 2
 LOW = jnp.bfloat16
 FF_BLOCK = 512
 D_BLOCK = 256
-SEND_PARTS = 4
+SEND_PARTS = 2
 MIB = 1 << 20
 
 inv_root_two = 0.7071067811865476
@@ -27,8 +30,16 @@
     return lax.axis_size(AXES)
 
 
-def exchange(blocks):
-    return lax.all_to_all(blocks, AXES, split_axis=0, concat_axis=0, tiled=True)
+def exchange(blocks, axes=AXES):
+    return lax.all_to_all(blocks, axes, split_axis=0, concat_axis=0, tiled=True)
+
+
+def swap_cores(block):
+    return lax.ppermute(block, "core", [(0, 1), (1, 0)])
+
+
+def core_index():
+    return lax.axis_index("core")
 
 
 def dot(a, b, dims):
@@ -41,10 +52,23 @@
 
 
 def route_kernel(
-    tokens, cotangent, keys, send, dispatch_out, combine_out, keys_hbm, keys_flat, sem
+    core,
+    tokens,
+    cotangent,
+    own,
+    other,
+    send,
+    dispatch_out,
+    combine_out,
+    keys_hbm,
+    keys,
+    keys_flat,
+    sem,
 ):
-    pairs = keys.shape[0]
+    pairs = send.shape[0]
     slots, width = keys_flat.shape
+    keys[:, core[0]] = own[...]
+    keys[:, CORES - 1 - core[0]] = other[...]
     keys_flat[...] = keys[...].reshape(slots, width)
     keep = pltpu.make_async_copy(keys_flat, keys_hbm, sem)
     keep.start()
@@ -81,19 +105,21 @@
 
 
 def logit_kernel(
+    core,
     back,
     tokens,
     cotangent,
     dispatch_in,
     combine_in,
-    send_hbm,
-    grad_low_out,
-    send,
+    own,
+    other,
+    grad_low_hbm,
+    terms,
+    grad_low,
     slot_out,
     grad_slot_in,
-    sems,
+    sem,
 ):
-    pairs, each, width = send.shape
     slot_out[...] = back[:, 0].reshape(slot_out.shape)
     grad_slot_in[...] = back[:, 1].reshape(slot_out.shape)
     dispatch = dispatch_in[...]
@@ -103,18 +129,23 @@
     grad_logits = dispatch * (
         grad_dispatch - jnp.sum(dispatch * grad_dispatch, axis=0, keepdims=True)
     ) + combine * (grad_combine - jnp.sum(combine * grad_combine, axis=1, keepdims=True))
-    grad_low = grad_logits.astype(LOW)
-    grad_low_out[...] = grad_low
-    terms = dot(grad_low, tokens[...], ((0,), (0,))).astype(LOW)
-    some = pairs // SEND_PARTS
+    grad_low[...] = grad_logits.astype(LOW)
+    keep = pltpu.make_async_copy(grad_low, grad_low_hbm, sem)
+    keep.start()
+    terms[...] = dot(grad_low[...], tokens[...], ((0,), (0,))).astype(LOW).reshape(terms.shape)
+    other[...] = terms[:, CORES - 1 - core[0]]
+    own[...] = terms[:, core[0]]
+    keep.wait()
+
+
+def add_kernel(own, other, sums_hbm, sums, sems):
+    some = sums.shape[0] // SEND_PARTS
     copies = []
     for j in range(SEND_PARTS):
         part = pl.ds(j * some, some)
-        send[part] = terms[j * some * each : (j + 1) * some * each].reshape(some, each, width)
-        copies.append(
-            pltpu.make_async_copy(send.at[part], send_hbm.at[part], sems.at[j])
-        )
-        copies[-1].start()
+        sums[part] = own[part] + other[part]
+        copies.append(pltpu.make_async_copy(sums.at[part], sums_hbm.at[part], sems.at[j]))
+        copies[j].start()
     for copy in copies:
         copy.wait()
 
@@ -145,6 +176,7 @@
 
 BESIDE = pl.CostEstimate(flops=20_000_000_000, bytes_accessed=1_000_000, transcendentals=0)
 VMEM = pl.BlockSpec(memory_space=pltpu.VMEM)
+SMEM = pl.BlockSpec(memory_space=pltpu.SMEM)
 HBM = pl.BlockSpec(memory_space=pltpu.HBM)
 
 
@@ -163,18 +195,21 @@
     slots = devices * SLOTS_EXP
     tokens, cotangent = tokens[0], cotangent[0]
     first_weight, second_weight = weight_in[0], weight_out[0]
-    pair_shape = (devices, SLOTS_EXP, width)
+    half_shape = (devices // CORES, SLOTS_EXP, width)
+    quad_shape = (devices // CORES, CORES, SLOTS_EXP, width)
+    core = core_index()[None]
     twin_shape = (devices, 2, SLOTS_EXP, width)
     send = pl.pallas_call(
         spread_kernel,
-        out_shape=shaped(LOW, *pair_shape),
+        out_shape=shaped(LOW, *half_shape),
         in_specs=[VMEM],
         out_specs=VMEM,
         cost_estimate=BESIDE,
         compiler_params=pltpu.CompilerParams(vmem_limit_bytes=4 * MIB),
         name="spread",
     )(slot_keys)
-    keys = exchange(send)
+    own_keys = exchange(send, ACROSS)
+    other_keys = swap_cores(own_keys)
 
     send, dispatch, combine, keys_all = pl.pallas_call(
         route_kernel,
@@ -184,13 +219,17 @@
             shaped(jnp.float32, length, slots),
             in_hbm(LOW, slots, width),
         ],
-        in_specs=[VMEM] * 3,
+        in_specs=[SMEM] + [VMEM] * 4,
         out_specs=[VMEM] * 3 + [HBM],
-        scratch_shapes=[pltpu.VMEM((slots, width), LOW), pltpu.SemaphoreType.DMA],
+        scratch_shapes=[
+            pltpu.VMEM(quad_shape, LOW),
+            pltpu.VMEM((slots, width), LOW),
+            pltpu.SemaphoreType.DMA,
+        ],
         cost_estimate=BESIDE,
         compiler_params=pltpu.CompilerParams(vmem_limit_bytes=8 * MIB),
         name="route",
-    )(tokens, cotangent, keys)
+    )(core, tokens, cotangent, own_keys, other_keys)
     arrived = exchange(send)
 
     rows = arrived.shape[0] * SLOTS_EXP
@@ -213,21 +252,35 @@
     back = exchange(send)
     grad_second = dot(hidden, grads, ((0,), (0,))).astype(LOW)
 
-    send, grad_low = pl.pallas_call(
+    own_terms, other_terms, grad_low = pl.pallas_call(
         logit_kernel,
-        out_shape=[in_hbm(LOW, *pair_shape), shaped(LOW, length, slots)],
-        in_specs=[VMEM] * 5,
-        out_specs=[HBM, VMEM],
+        out_shape=[
+            shaped(LOW, *half_shape),
+            shaped(LOW, *half_shape),
+            in_hbm(LOW, length, slots),
+        ],
+        in_specs=[SMEM] + [VMEM] * 5,
+        out_specs=[VMEM, VMEM, HBM],
         scratch_shapes=[
-            pltpu.VMEM(pair_shape, LOW),
+            pltpu.VMEM(quad_shape, LOW),
+            pltpu.VMEM((length, slots), LOW),
             pltpu.VMEM((slots, width), LOW),
             pltpu.VMEM((slots, width), LOW),
-            pltpu.SemaphoreType.DMA((SEND_PARTS,)),
+            pltpu.SemaphoreType.DMA,
         ],
         compiler_params=pltpu.CompilerParams(vmem_limit_bytes=8 * MIB),
         name="logit",
-    )(back, tokens, cotangent, dispatch, combine)
-    terms = exchange(send)
+    )(core, back, tokens, cotangent, dispatch, combine)
+    send = pl.pallas_call(
+        add_kernel,
+        out_shape=in_hbm(LOW, *half_shape),
+        in_specs=[VMEM] * 2,
+        out_specs=HBM,
+        scratch_shapes=[pltpu.VMEM(half_shape, LOW), pltpu.SemaphoreType.DMA((SEND_PARTS,))],
+        compiler_params=pltpu.CompilerParams(vmem_limit_bytes=4 * MIB),
+        name="add",
+    )(own_terms, swap_cores(other_terms))
+    terms = exchange(send, ACROSS)
     mixed_out, grad_tokens = pl.pallas_call(
         finish_kernel,
         out_shape=[shaped(LOW, length, width)] * 2,
@@ -249,6 +302,8 @@
 
 
 def solution(mesh):
+    groups, members = mesh.devices.shape
+    mesh = Mesh(mesh.devices.reshape(groups, members // CORES, CORES), AXES)
     in_specs = (
         P(AXES, None, None),
         P(AXES, None),

time: 111 us -> 108 us (0.973)
  blocking collectives: 78.1 us -> 73 us
  starting transfers between devices: 4.31 us -> 7.48 us
  waiting for transfers between devices: 7.38 us -> 5.52 us
    all_to_all x3, blocking collectives: 78.1 us -> 73 us  [exchange(): return lax.all_to_all(blocks, axes, split_axis=0, concat_axis=0, tiled=True)]
    all_to_all x1, waiting for transfers between devices: 7.38 us -> 2.65 us  [exchange(): return lax.all_to_all(blocks, axes, split_axis=0, concat_axis=0, tiled=True)]
    ppermute x0 -> x2, waiting for transfers between devices: none -> 2.87 us  [swap_cores(): return lax.ppermute(block, 'core', [(0, 1), (1, 0)])]
    ppermute x0 -> x2, starting transfers between devices: none -> 2.41 us  [swap_cores(): return lax.ppermute(block, 'core', [(0, 1), (1, 0)])]
    pallas_call x2 -> x3, Pallas kernels: 1.99 us -> 2.25 us  [the longest x1 1.45 us: local(): pl.pallas_call(logit_kernel, out_shape=[shaped(LOW, *half_shape), shaped(...]
  transfers between devices with their start and end apart: 1 -> 3, of which waited for: 1 -> 3; matrix products, arithmetic and copies ran while one was open for 5% -> 6% of each run, Pallas kernels for 1% -> 1%
where the time goes in v4:
time: 108 us; the launch traced here: 107 us
  blocking collectives  73 us (68%)
  Pallas kernels  13.2 us (12%)
  starting transfers between devices  7.48 us (7%)
  matrix products  5.87 us (5%)
  waiting for transfers between devices  5.52 us (5%)
    all_to_all x3, blocking collectives, exchange(): return lax.all_to_all(blocks, axes, split_axis=0, concat_axis=0, tiled=True)  73 us
    pallas_call x1, Pallas kernels, local(): pl.pallas_call(expert_kernel, out_shape=[shaped(LOW, *twin_shape), shaped...  7.13 us
    dot_general x1, matrix products, dot(): lax.dot_general(a, b, (dims, ((), ())), preferred_element_type=jnp.float32)  5.87 us
    all_to_all x1, starting transfers between devices, exchange(): return lax.all_to_all(blocks, axes, split_axis=0, concat_axis=0, tiled=True)  5.07 us
    ppermute x2, waiting for transfers between devices, swap_cores(): return lax.ppermute(block, 'core', [(0, 1), (1, 0)])  2.87 us
    all_to_all x1, waiting for transfers between devices, exchange(): return lax.all_to_all(blocks, axes, split_axis=0, concat_axis=0, tiled=True)  2.65 us
    ppermute x2, starting transfers between devices, swap_cores(): return lax.ppermute(block, 'core', [(0, 1), (1, 0)])  2.41 us
  transfers between devices with their start and end apart: 3, of which 3 were waited for; matrix products, arithmetic and copies ran while one was open for 6% of the time, Pallas kernels for 1%

profile of v4, /device:TPU:1, one launch (start us, length us, event | category | flops | bytes accessed | tf_op | source)
XLA Modules:
  0.0 106.7 jit_solution(3886272236122252221)
XLA Ops:
  0.6 0.0 copy-start.4
  0.6 0.0 copy-start.2
  0.7 0.0 copy-start.7
  0.7 0.8 copy-done.7
  1.5 21.6 %all_to_all.20.own = bf16[64,2,1280]{2,1,0:T(2,128)(2,1)S(1)} all-to-all(bf16[64,2,1280]{2,1,0:T(2,128)(2,1)S(1)} %spread.1), channel_id=1, replica_groups=mesh['dp'=8,'chip'=8,'core'=2] {'dp','chip'}, dimensions={0} | all-to-all | bytes 655360 | tf_op jit(solution)/shard_map/all_to_all | solution.py:34
  23.0 2.3 %collective-permute-start = (bf16[64,2,1280]{2,1,0:T(2,128)(2,1)S(1)}, bf16[64,2,1280]{2,1,0:T(2,128)(2,1)S(1)}, u32[]{:S(2)}, u32[]{:S(2)}) collective-permute-start(bf16[64,2,1280]{2,1,0:T(2,128)(2,1)S(1)} %all_to_all.20.own), channel_id=1, source_target_pairs={{0,1},{1,0},{2,3},{3,2},{4,5},{5,4},{6,7},{7,6},{8,9},{9,8},{10,11... | collective-permute-start | bytes 983048 | tf_op jit(solution)/shard_map/ppermute | solution.py:38
  25.4 1.3 %collective-permute-done.other = bf16[64,2,1280]{2,1,0:T(2,128)(2,1)S(1)} collective-permute-done((bf16[64,2,1280]{2,1,0:T(2,128)(2,1)S(1)}, bf16[64,2,1280]{2,1,0:T(2,128)(2,1)S(1)}, u32[]{:S(2)}, u32[]{:S(2)}) %collective-permute-start) | collective-permute-done | bytes 327712 | tf_op jit(solution)/shard_map/ppermute | solution.py:38
  26.6 0.0 slice-start
  26.6 0.0 slice-start.2
  26.6 0.0 copy-done.4
  26.6 0.0 copy-done.2
  26.6 0.0 slice-start.1
  26.6 0.0 slice-start.3
  26.7 1.4 %route.1 = (bf16[128,2,2,1280]{3,2,1,0:T(2,128)(2,1)S(1)}, f32[256,256]{1,0:T(8,128)S(1)}, f32[256,256]{1,0:T(8,128)S(1)}, bf16[256,1280]{1,0:T(8,128)(2,1)}) custom-call(s32[1]{0:T(128)} %bitcast.core, bf16[256,1280]{1,0:T(8,128)(2,1)S(1)} %bitcast.17, bf16[256,1280]{1,0:T(8,128)(2,1)S(1)} %bitcast.19, bf16[64,2,1280]{2,1,0:T(2,128)(2,1)S(1)} %all_to_all.20.own, ...), custom_call_target="tpu_custom_call" | custom-call | flops 20000000000 | bytes 1000000 | tf_op jit(solution)/shard_map/route/pallas_call | solution.py:214
  28.1 25.5 %all_to_all.21.arrived = bf16[128,2,2,1280]{3,2,1,0:T(2,128)(2,1)S(1)} all-to-all(bf16[128,2,2,1280]{3,2,1,0:T(2,128)(2,1)S(1)} %get-tuple-element.16), channel_id=1, replica_groups=mesh['dp'=8,'chip'=8,'core'=2] {'dp','chip','core'}, dimensions={0} | all-to-all | bytes 2621440 | tf_op jit(solution)/shard_map/all_to_all | solution.py:34
  53.6 0.0 slice-done
  53.6 0.0 slice-done.2
  53.6 0.0 slice-done.1
  53.6 0.0 slice-done.3
  53.6 7.1 %expert.1 = (bf16[128,2,2,1280]{3,2,1,0:T(2,128)(2,1)S(1)}, bf16[256,2560]{1,0:T(8,128)(2,1)S(1)}, bf16[256,1280]{1,0:T(8,128)(2,1)S(1)}) custom-call(bf16[128,2,2,1280]{3,2,1,0:T(2,128)(2,1)S(1)} %all_to_all.21.arrived, bf16[1280,2560]{1,0:T(8,128)(2,1)S(1)} %bitcast.13, bf16[2560,1280]{1,0:T(8,128)(2,1)S(1)} %bitcast.16), custom_call_target="tpu_custom_call" | custom-call | tf_op jit(solution)/shard_map/expert/pallas_call | solution.py:236
  60.8 0.0 copy-start
  60.8 0.0 copy-start.3
  60.8 0.0 copy-start.5
  60.8 26.0 %all_to_all.22.back = bf16[128,2,2,1280]{3,2,1,0:T(2,128)(2,1)S(1)} all-to-all(bf16[128,2,2,1280]{3,2,1,0:T(2,128)(2,1)S(1)} %get-tuple-element.17), channel_id=1, replica_groups=mesh['dp'=8,'chip'=8,'core'=2] {'dp','chip','core'}, dimensions={0} | all-to-all | bytes 2621440 | tf_op jit(solution)/shard_map/all_to_all | solution.py:34
  86.8 0.0 copy-done
  86.8 0.0 copy-done.3
  86.8 0.0 copy-done.5
  86.8 1.5 %logit.1 = (bf16[64,2,1280]{2,1,0:T(2,128)(2,1)S(1)}, bf16[64,2,1280]{2,1,0:T(2,128)(2,1)S(1)}, bf16[256,256]{1,0:T(8,128)(2,1)}) custom-call(s32[1]{0:T(128)} %bitcast.core, bf16[128,2,2,1280]{3,2,1,0:T(2,128)(2,1)S(1)} %all_to_all.22.back, bf16[256,1280]{1,0:T(8,128)(2,1)S(1)} %bitcast.18, bf16[256,1280]{1,0:T(8,128)(2,1)S(1)} %bitcast.20, ...), custom_call_target="tpu_custom_call" | custom-call | tf_op jit(solution)/shard_map/logit/pallas_call | solution.py:255
  88.2 0.1 collective-permute-start.1
  88.3 1.6 %collective-permute-done.1.other = bf16[64,2,1280]{2,1,0:T(2,128)(2,1)S(1)} collective-permute-done((bf16[64,2,1280]{2,1,0:T(2,128)(2,1)S(1)}, bf16[64,2,1280]{2,1,0:T(2,128)(2,1)S(1)}, u32[]{:S(2)}, u32[]{:S(2)}) %collective-permute-start.1) | collective-permute-done | bytes 327712 | tf_op jit(solution)/shard_map/ppermute | solution.py:38
  89.9 0.8 add.1
  90.7 5.1 %all-to-all-start.3 = ((bf16[64,2,1280]{2,1,0:T(2,128)(2,1)}), bf16[64,2,1280]{2,1,0:T(2,128)(2,1)S(1)}, u32[]{:S(2)}, u32[]{:S(2)}) async-start(bf16[64,2,1280]{2,1,0:T(2,128)(2,1)} %add.1), calls=%async_computation.3 | async-start | bytes 655360 | tf_op jit(solution)/shard_map/all_to_all | solution.py:34
  95.8 0.0 copy-start.1
  95.8 0.0 copy-start.6
  95.8 5.9 %fusion = bf16[1,2560,1280]{2,1,0:T(8,128)(2,1)} fusion(bf16[256,2560]{1,0:T(8,128)(2,1)S(1)} %get-tuple-element.26, bf16[256,1280]{1,0:T(8,128)(2,1)} %copy-done), kind=kOutput, calls=%fused_computation.1 | convolution fusion | flops 1680998400 | bytes 8519680 | tf_op jit(solution)/shard_map/dot_general | solution.py:46
  101.7 0.0 copy-done.1
  101.7 0.0 copy-done.6
  101.7 1.6 %finish.1 = (bf16[256,1280]{1,0:T(8,128)(2,1)}, bf16[256,1280]{1,0:T(8,128)(2,1)}) custom-call(bf16[128,2,2,1280]{3,2,1,0:T(2,128)(2,1)S(1)} %all_to_all.22.back, f32[256,256]{1,0:T(8,128)S(1)} %get-tuple-element.18.dispatch_in.dispatch, f32[256,256]{1,0:T(8,128)S(1)} %get-tuple-element.19.combine_in.combine, bf16[256,256]{1,0:T(8,128)(2,1)S(1)} %copy-done.6, ...), custom_call_target="tpu_custom_call" | custom-call | tf_op jit(solution)/shard_map/finish/pallas_call | solution.py:284
  103.3 2.6 %all-to-all-done.3.terms = bf16[64,2,1280]{2,1,0:T(2,128)(2,1)S(1)} async-done(((bf16[64,2,1280]{2,1,0:T(2,128)(2,1)}), bf16[64,2,1280]{2,1,0:T(2,128)(2,1)S(1)}, u32[]{:S(2)}, u32[]{:S(2)}) %all-to-all-start.3) | async-done | bytes 327712 | tf_op jit(solution)/shard_map/all_to_all | solution.py:34
  105.9 0.8 total.1
  (3 shorter events, 0.0 us)
Async XLA Ops:
  0.6 26.0 %copy-start.4 = (bf16[1,256,1280]{2,1,0:T(8,128)(2,1)S(1)}, bf16[1,256,1280]{2,1,0:T(8,128)(2,1)}, u32[]{:S(2)}) copy-start(bf16[1,256,1280]{2,1,0:T(8,128)(2,1)} %param.9) | copy-start | bytes 1966084
  0.6 26.0 %copy-start.2 = (bf16[1,256,1280]{2,1,0:T(8,128)(2,1)S(1)}, bf16[1,256,1280]{2,1,0:T(8,128)(2,1)}, u32[]{:S(2)}) copy-start(bf16[1,256,1280]{2,1,0:T(8,128)(2,1)} %param.5) | copy-start | bytes 1966084
  0.7 0.8 copy-start.7
  23.0 3.6 %collective-permute-start = (bf16[64,2,1280]{2,1,0:T(2,128)(2,1)S(1)}, bf16[64,2,1280]{2,1,0:T(2,128)(2,1)S(1)}, u32[]{:S(2)}, u32[]{:S(2)}) collective-permute-start(bf16[64,2,1280]{2,1,0:T(2,128)(2,1)S(1)} %all_to_all.20.own), channel_id=1, source_target_pairs={{0,1},{1,0},{2,3},{3,2},{4,5},{5,4},{6,7},{7,6},{8,9},{9,8},{10,11... | collective-permute-start | bytes 983048 | tf_op jit(solution)/shard_map/ppermute | solution.py:38
  26.6 27.0 %slice-start = ((s8[6553600]{0:T(1024)(128)(4,1)}), s8[4194304]{0:T(1024)(128)(4,1)S(1)}, s32[]{:S(2)}) async-start(s8[6553600]{0:T(1024)(128)(4,1)} %bitcast.11), calls=%async_computation.4 | async-start | bytes 8388608
  26.6 27.0 %slice-start.2 = ((s8[6553600]{0:T(1024)(128)(4,1)}), s8[4194304]{0:T(1024)(128)(4,1)S(1)}, s32[]{:S(2)}) async-start(s8[6553600]{0:T(1024)(128)(4,1)} %bitcast.14), calls=%async_computation.6 | async-start | bytes 8388608
  26.6 27.0 %slice-start.1 = ((s8[6553600]{0:T(1024)(128)(4,1)}), s8[2359296]{0:T(1024)(128)(4,1)S(1)}, s32[]{:S(2)}) async-start(s8[6553600]{0:T(1024)(128)(4,1)} %bitcast.11), calls=%async_computation.5 | async-start | bytes 4718592
  26.6 26.9 %slice-start.3 = ((s8[6553600]{0:T(1024)(128)(4,1)}), s8[2359296]{0:T(1024)(128)(4,1)S(1)}, s32[]{:S(2)}) async-start(s8[6553600]{0:T(1024)(128)(4,1)} %bitcast.14), calls=%async_computation.7 | async-start | bytes 4718592
  60.8 26.0 %copy-start = (bf16[256,1280]{1,0:T(8,128)(2,1)}, bf16[256,1280]{1,0:T(8,128)(2,1)S(1)}, u32[]{:S(2)}) copy-start(bf16[256,1280]{1,0:T(8,128)(2,1)S(1)} %get-tuple-element.27) | copy-start | bytes 1966084
  60.8 26.0 %copy-start.3 = (bf16[1,256,1280]{2,1,0:T(8,128)(2,1)S(1)}, bf16[1,256,1280]{2,1,0:T(8,128)(2,1)}, u32[]{:S(2)}) copy-start(bf16[1,256,1280]{2,1,0:T(8,128)(2,1)} %param.5) | copy-start | bytes 1966084
  60.8 26.0 %copy-start.5 = (bf16[1,256,1280]{2,1,0:T(8,128)(2,1)S(1)}, bf16[1,256,1280]{2,1,0:T(8,128)(2,1)}, u32[]{:S(2)}) copy-start(bf16[1,256,1280]{2,1,0:T(8,128)(2,1)} %param.9) | copy-start | bytes 1966084
  88.2 1.7 %collective-permute-start.1 = (bf16[64,2,1280]{2,1,0:T(2,128)(2,1)S(1)}, bf16[64,2,1280]{2,1,0:T(2,128)(2,1)S(1)}, u32[]{:S(2)}, u32[]{:S(2)}) collective-permute-start(bf16[64,2,1280]{2,1,0:T(2,128)(2,1)S(1)} %get-tuple-element.25), channel_id=1, source_target_pairs={{0,1},{1,0},{2,3},{3,2},{4,5},{5,4},{6,7},{7,6},{8,9},{9,8},{10,11... | collective-permute-start | bytes 983048 | tf_op jit(solution)/shard_map/ppermute | solution.py:38
  90.7 15.2 %all-to-all-start.3 = ((bf16[64,2,1280]{2,1,0:T(2,128)(2,1)}), bf16[64,2,1280]{2,1,0:T(2,128)(2,1)S(1)}, u32[]{:S(2)}, u32[]{:S(2)}) async-start(bf16[64,2,1280]{2,1,0:T(2,128)(2,1)} %add.1), calls=%async_computation.3 | async-start | bytes 655360 | tf_op jit(solution)/shard_map/all_to_all | solution.py:34
  95.8 5.9 %copy-start.1 = (bf16[256,1280]{1,0:T(8,128)(2,1)S(1)}, bf16[256,1280]{1,0:T(8,128)(2,1)}, u32[]{:S(2)}) copy-start(bf16[256,1280]{1,0:T(8,128)(2,1)} %get-tuple-element.21.keys) | copy-start | bytes 1966084
  95.8 5.9 %copy-start.6 = (bf16[256,256]{1,0:T(8,128)(2,1)S(1)}, bf16[256,256]{1,0:T(8,128)(2,1)}, u32[]{:S(2)}) copy-start(bf16[256,256]{1,0:T(8,128)(2,1)} %get-tuple-element.20.grad_low) | copy-start | bytes 393220

commit v5 on v4

--- a/solution.py
+++ b/solution.py
@@ -84,14 +84,17 @@
     keep.wait()
 
 
-def expert_kernel(arrived, first, second, send, hidden, grads, rows, grad_pre):
+def expert_kernel(arrived, first, second, send, hidden, grads_hbm, rows, grads, grad_pre, sem):
     width, inner = first.shape
     pairs = arrived.shape[0]
     rows[...] = arrived[:, 0].reshape(rows.shape)
-    grads[...] = arrived[:, 1].reshape(rows.shape)
     for i in range(inner // FF_BLOCK):
         block = pl.ds(i * FF_BLOCK, FF_BLOCK)
         pre_act = dot(rows[...], first[:, block], ((1,), (0,)))
+        if i == 0:
+            grads[...] = arrived[:, 1].reshape(rows.shape)
+            keep = pltpu.make_async_copy(grads, grads_hbm, sem)
+            keep.start()
         grad_hidden = dot(grads[...], second[block, :], ((1,), (1,)))
         active, slope = gelu_pair(pre_act)
         hidden[:, block] = active.astype(LOW)
@@ -102,6 +105,7 @@
         send[:, 0, :, block] = out.reshape(pairs, SLOTS_EXP, D_BLOCK)
         back = dot(grad_pre[...], first[block, :], ((1,), (1,))).astype(LOW)
         send[:, 1, :, block] = back.reshape(pairs, SLOTS_EXP, D_BLOCK)
+    keep.wait()
 
 
 def logit_kernel(
@@ -151,14 +155,58 @@
 
 
 def finish_kernel(
-    back, dispatch, combine, grad_low, keys, mixed_out, grad_tokens, slot_out, grad_slot_in
+    back,
+    dispatch,
+    combine,
+    hidden,
+    grad_low_hbm,
+    keys_hbm,
+    grads_hbm,
+    mixed_hbm,
+    grad_tokens_hbm,
+    grad_second_hbm,
+    slot_out,
+    grad_slot_in,
+    grad_low,
+    keys,
+    grads,
+    mixed_out,
+    grad_tokens,
+    blocks,
+    sems,
 ):
+    arrivals = [
+        pltpu.make_async_copy(grad_low_hbm, grad_low, sems.at[5]),
+        pltpu.make_async_copy(keys_hbm, keys, sems.at[6]),
+        pltpu.make_async_copy(grads_hbm, grads, sems.at[0]),
+    ]
+    for arrival in arrivals:
+        arrival.start()
     slot_out[...] = back[:, 0].reshape(slot_out.shape)
     mixed_out[...] = dot(combine[...].astype(LOW), slot_out[...], ((1,), (0,))).astype(LOW)
+    leave_mixed = pltpu.make_async_copy(mixed_out, mixed_hbm, sems.at[1])
+    leave_mixed.start()
     grad_slot_in[...] = back[:, 1].reshape(slot_out.shape)
     through_slots = dot(dispatch[...].astype(LOW), grad_slot_in[...], ((1,), (0,)))
+    arrivals[0].wait()
+    arrivals[1].wait()
     through_keys = dot(grad_low[...], keys[...], ((1,), (0,)))
     grad_tokens[...] = (through_slots + through_keys).astype(LOW)
+    leave_tokens = pltpu.make_async_copy(grad_tokens, grad_tokens_hbm, sems.at[2])
+    leave_tokens.start()
+    arrivals[2].wait()
+    copies = []
+    for i in range(hidden.shape[1] // FF_BLOCK):
+        if i >= 2:
+            copies[i - 2].wait()
+        block = pl.ds(i * FF_BLOCK, FF_BLOCK)
+        blocks[i % 2] = dot(hidden[:, block], grads[...], ((0,), (0,))).astype(LOW)
+        copies.append(
+            pltpu.make_async_copy(blocks.at[i % 2], grad_second_hbm.at[block], sems.at[3 + i % 2])
+        )
+        copies[i].start()
+    for copy in (leave_mixed, leave_tokens, *copies[-2:]):
+        copy.wait()
 
 
 def sum_kernel(terms, total):
@@ -170,7 +218,10 @@
     total[...] = dot(chosen, flat, ((1,), (0,)))[0:each]
 
 
-def spread_kernel(keys, send):
+def spread_kernel(keys_hbm, send, keys, sem):
+    copy = pltpu.make_async_copy(keys_hbm, keys, sem)
+    copy.start()
+    copy.wait()
     send[...] = jnp.broadcast_to(keys[...][None], send.shape)
 
 
@@ -182,6 +233,10 @@
 
 def in_hbm(dtype, *shape):
     return pltpu.HBM(shape, dtype)
+
+
+def stay(array):
+    return pltpu.with_memory_space_constraint(array, pltpu.HBM)
 
 
 def shaped(dtype, *shape):
@@ -202,12 +257,13 @@
     send = pl.pallas_call(
         spread_kernel,
         out_shape=shaped(LOW, *half_shape),
-        in_specs=[VMEM],
+        in_specs=[HBM],
         out_specs=VMEM,
+        scratch_shapes=[pltpu.VMEM((SLOTS_EXP, width), LOW), pltpu.SemaphoreType.DMA],
         cost_estimate=BESIDE,
         compiler_params=pltpu.CompilerParams(vmem_limit_bytes=4 * MIB),
         name="spread",
-    )(slot_keys)
+    )(stay(slot_keys))
     own_keys = exchange(send, ACROSS)
     other_keys = swap_cores(own_keys)
 
@@ -238,19 +294,20 @@
         out_shape=[
             shaped(LOW, *twin_shape),
             shaped(LOW, rows, inner),
-            shaped(LOW, rows, width),
+            in_hbm(LOW, rows, width),
         ],
         in_specs=[VMEM] * 3,
-        out_specs=[VMEM] * 3,
+        out_specs=[VMEM] * 2 + [HBM],
         scratch_shapes=[
             pltpu.VMEM((rows, width), LOW),
+            pltpu.VMEM((rows, width), LOW),
             pltpu.VMEM((rows, inner), LOW),
+            pltpu.SemaphoreType.DMA,
         ],
         compiler_params=pltpu.CompilerParams(vmem_limit_bytes=10 * MIB),
         name="expert",
     )(arrived, first_weight, second_weight)
     back = exchange(send)
-    grad_second = dot(hidden, grads, ((0,), (0,))).astype(LOW)
 
     own_terms, other_terms, grad_low = pl.pallas_call(
         logit_kernel,
@@ -281,15 +338,29 @@
         name="add",
     )(own_terms, swap_cores(other_terms))
     terms = exchange(send, ACROSS)
-    mixed_out, grad_tokens = pl.pallas_call(
+    mixed_out, grad_tokens, grad_second = pl.pallas_call(
         finish_kernel,
-        out_shape=[shaped(LOW, length, width)] * 2,
-        in_specs=[VMEM] * 5,
-        out_specs=[VMEM] * 2,
-        scratch_shapes=[pltpu.VMEM((slots, width), LOW)] * 2,
-        compiler_params=pltpu.CompilerParams(vmem_limit_bytes=8 * MIB),
+        out_shape=[
+            in_hbm(LOW, length, width),
+            in_hbm(LOW, length, width),
+            in_hbm(LOW, inner, width),
+        ],
+        in_specs=[VMEM] * 4 + [HBM] * 3,
+        out_specs=[HBM] * 3,
+        scratch_shapes=[
+            pltpu.VMEM((slots, width), LOW),
+            pltpu.VMEM((slots, width), LOW),
+            pltpu.VMEM((length, slots), LOW),
+            pltpu.VMEM((slots, width), LOW),
+            pltpu.VMEM((rows, width), LOW),
+            pltpu.VMEM((length, width), LOW),
+            pltpu.VMEM((length, width), LOW),
+            pltpu.VMEM((2, FF_BLOCK, width), LOW),
+            pltpu.SemaphoreType.DMA((7,)),
+        ],
+        compiler_params=pltpu.CompilerParams(vmem_limit_bytes=16 * MIB),
         name="finish",
-    )(back, dispatch, combine, grad_low, keys_all)
+    )(back, dispatch, combine, hidden, stay(grad_low), stay(keys_all), stay(grads))
     grad_keys = pl.pallas_call(
         sum_kernel,
         out_shape=shaped(jnp.float32, SLOTS_EXP, width),

time: 108 us -> 108 us (level)
  Pallas kernels: 13.2 us -> 19.1 us
  matrix products: 5.87 us -> 0 us
    dot_general x1 -> x0, matrix products: 5.87 us -> none  [dot(): lax.dot_general(a, b, (dims, ((), ())), preferred_element_type=jnp.float32)]
    pallas_call x1, Pallas kernels: 1.6 us -> 6.77 us  [local(): pl.pallas_call(finish_kernel, out_shape=[in_hbm(LOW, length, width), in_h...]
  transfers between devices with their start and end apart: 3 -> 3, of which waited for: 3 -> 3; matrix products, arithmetic and copies ran while one was open for 6% -> 0% of each run, Pallas kernels for 1% -> 6%
where the time goes in v5:
time: 108 us; the launch traced here: 107 us
  blocking collectives  73 us (68%)
  Pallas kernels  19.1 us (18%)
  starting transfers between devices  7.48 us (7%)
  waiting for transfers between devices  6.24 us (6%)
    all_to_all x3, blocking collectives, exchange(): return lax.all_to_all(blocks, axes, split_axis=0, concat_axis=0, tiled=True)  73 us
    pallas_call x1, Pallas kernels, local(): pl.pallas_call(expert_kernel, out_shape=[shaped(LOW, *twin_shape), shaped...  7.16 us
    pallas_call x1, Pallas kernels, local(): pl.pallas_call(finish_kernel, out_shape=[in_hbm(LOW, length, width), in_h...  6.77 us
    all_to_all x1, starting transfers between devices, exchange(): return lax.all_to_all(blocks, axes, split_axis=0, concat_axis=0, tiled=True)  5.08 us
    all_to_all x1, waiting for transfers between devices, exchange(): return lax.all_to_all(blocks, axes, split_axis=0, concat_axis=0, tiled=True)  3.37 us
    ppermute x2, waiting for transfers between devices, swap_cores(): return lax.ppermute(block, 'core', [(0, 1), (1, 0)])  2.87 us
    ppermute x2, starting transfers between devices, swap_cores(): return lax.ppermute(block, 'core', [(0, 1), (1, 0)])  2.41 us
  transfers between devices with their start and end apart: 3, of which 3 were waited for; matrix products, arithmetic and copies ran while one was open for 0% of the time, Pallas kernels for 6%

profile of v5, /device:TPU:1, one launch (start us, length us, event | category | flops | bytes accessed | tf_op | source)
XLA Modules:
  0.0 106.7 jit_solution(11662712303626989061)
XLA Ops:
  0.6 0.0 copy-start.2
  0.6 0.0 copy-start
  0.7 0.8 spread.1
  1.5 21.6 %all_to_all.20.own = bf16[64,2,1280]{2,1,0:T(2,128)(2,1)S(1)} all-to-all(bf16[64,2,1280]{2,1,0:T(2,128)(2,1)S(1)} %spread.1), channel_id=1, replica_groups=mesh['dp'=8,'chip'=8,'core'=2] {'dp','chip'}, dimensions={0} | all-to-all | bytes 655360 | tf_op jit(solution)/shard_map/all_to_all | solution.py:34
  23.1 2.3 %collective-permute-start = (bf16[64,2,1280]{2,1,0:T(2,128)(2,1)S(1)}, bf16[64,2,1280]{2,1,0:T(2,128)(2,1)S(1)}, u32[]{:S(2)}, u32[]{:S(2)}) collective-permute-start(bf16[64,2,1280]{2,1,0:T(2,128)(2,1)S(1)} %all_to_all.20.own), channel_id=1, source_target_pairs={{0,1},{1,0},{2,3},{3,2},{4,5},{5,4},{6,7},{7,6},{8,9},{9,8},{10,11... | collective-permute-start | bytes 983048 | tf_op jit(solution)/shard_map/ppermute | solution.py:38
  25.4 1.3 %collective-permute-done.other = bf16[64,2,1280]{2,1,0:T(2,128)(2,1)S(1)} collective-permute-done((bf16[64,2,1280]{2,1,0:T(2,128)(2,1)S(1)}, bf16[64,2,1280]{2,1,0:T(2,128)(2,1)S(1)}, u32[]{:S(2)}, u32[]{:S(2)}) %collective-permute-start) | collective-permute-done | bytes 327712 | tf_op jit(solution)/shard_map/ppermute | solution.py:38
  26.6 0.0 slice-start
  26.6 0.0 slice-start.2
  26.6 0.0 copy-done.2
  26.6 0.0 copy-done
  26.6 0.0 slice-start.1
  26.7 0.0 slice-start.3
  26.7 1.4 %route.1 = (bf16[128,2,2,1280]{3,2,1,0:T(2,128)(2,1)S(1)}, f32[256,256]{1,0:T(8,128)S(1)}, f32[256,256]{1,0:T(8,128)S(1)}, bf16[256,1280]{1,0:T(8,128)(2,1)}) custom-call(s32[1]{0:T(128)} %bitcast.core, bf16[256,1280]{1,0:T(8,128)(2,1)S(1)} %bitcast.14, bf16[256,1280]{1,0:T(8,128)(2,1)S(1)} %bitcast.16, bf16[64,2,1280]{2,1,0:T(2,128)(2,1)S(1)} %all_to_all.20.own, ...), custom_call_target="tpu_custom_call" | custom-call | flops 20000000000 | bytes 1000000 | tf_op jit(solution)/shard_map/route/pallas_call | solution.py:270
  28.1 25.5 %all_to_all.21.arrived = bf16[128,2,2,1280]{3,2,1,0:T(2,128)(2,1)S(1)} all-to-all(bf16[128,2,2,1280]{3,2,1,0:T(2,128)(2,1)S(1)} %get-tuple-element.17), channel_id=1, replica_groups=mesh['dp'=8,'chip'=8,'core'=2] {'dp','chip','core'}, dimensions={0} | all-to-all | bytes 2621440 | tf_op jit(solution)/shard_map/all_to_all | solution.py:34
  53.6 0.0 slice-done
  53.6 0.0 slice-done.2
  53.6 0.0 slice-done.1
  53.6 0.0 slice-done.3
  53.6 7.2 %expert.1 = (bf16[128,2,2,1280]{3,2,1,0:T(2,128)(2,1)S(1)}, bf16[256,2560]{1,0:T(8,128)(2,1)S(1)}, bf16[256,1280]{1,0:T(8,128)(2,1)}) custom-call(bf16[128,2,2,1280]{3,2,1,0:T(2,128)(2,1)S(1)} %all_to_all.21.arrived, bf16[1280,2560]{1,0:T(8,128)(2,1)S(1)} %bitcast.10, bf16[2560,1280]{1,0:T(8,128)(2,1)S(1)} %bitcast.13), custom_call_target="tpu_custom_call" | custom-call | tf_op jit(solution)/shard_map/expert/pallas_call | solution.py:292
  60.8 0.0 copy-start.1
  60.8 0.0 copy-start.3
  60.8 26.0 %all_to_all.22.back = bf16[128,2,2,1280]{3,2,1,0:T(2,128)(2,1)S(1)} all-to-all(bf16[128,2,2,1280]{3,2,1,0:T(2,128)(2,1)S(1)} %get-tuple-element.18), channel_id=1, replica_groups=mesh['dp'=8,'chip'=8,'core'=2] {'dp','chip','core'}, dimensions={0} | all-to-all | bytes 2621440 | tf_op jit(solution)/shard_map/all_to_all | solution.py:34
  86.8 0.0 copy-done.1
  86.8 0.0 copy-done.3
  86.8 1.5 %logit.1 = (bf16[64,2,1280]{2,1,0:T(2,128)(2,1)S(1)}, bf16[64,2,1280]{2,1,0:T(2,128)(2,1)S(1)}, bf16[256,256]{1,0:T(8,128)(2,1)}) custom-call(s32[1]{0:T(128)} %bitcast.core, bf16[128,2,2,1280]{3,2,1,0:T(2,128)(2,1)S(1)} %all_to_all.22.back, bf16[256,1280]{1,0:T(8,128)(2,1)S(1)} %bitcast.15, bf16[256,1280]{1,0:T(8,128)(2,1)S(1)} %bitcast.17, ...), custom_call_target="tpu_custom_call" | custom-call | tf_op jit(solution)/shard_map/logit/pallas_call | solution.py:312
  88.3 0.1 collective-permute-start.1
  88.3 1.6 %collective-permute-done.1.other = bf16[64,2,1280]{2,1,0:T(2,128)(2,1)S(1)} collective-permute-done((bf16[64,2,1280]{2,1,0:T(2,128)(2,1)S(1)}, bf16[64,2,1280]{2,1,0:T(2,128)(2,1)S(1)}, u32[]{:S(2)}, u32[]{:S(2)}) %collective-permute-start.1) | collective-permute-done | bytes 327712 | tf_op jit(solution)/shard_map/ppermute | solution.py:38
  90.0 0.8 add.1
  90.7 5.1 %all-to-all-start.3 = ((bf16[64,2,1280]{2,1,0:T(2,128)(2,1)}), bf16[64,2,1280]{2,1,0:T(2,128)(2,1)S(1)}, u32[]{:S(2)}, u32[]{:S(2)}) async-start(bf16[64,2,1280]{2,1,0:T(2,128)(2,1)} %add.1), calls=%async_computation.3 | async-start | bytes 655360 | tf_op jit(solution)/shard_map/all_to_all | solution.py:34
  95.8 6.8 %finish.1 = (bf16[256,1280]{1,0:T(8,128)(2,1)}, bf16[256,1280]{1,0:T(8,128)(2,1)}, bf16[2560,1280]{1,0:T(8,128)(2,1)}) custom-call(bf16[128,2,2,1280]{3,2,1,0:T(2,128)(2,1)S(1)} %all_to_all.22.back, f32[256,256]{1,0:T(8,128)S(1)} %get-tuple-element.19.dispatch_in.dispatch, f32[256,256]{1,0:T(8,128)S(1)} %get-tuple-element.20.combine_in.combine, ...), custom_call_target="tpu_custom_call" | custom-call | tf_op jit(solution)/shard_map/finish/pallas_call | solution.py:341
  102.6 3.4 %all-to-all-done.3.terms = bf16[64,2,1280]{2,1,0:T(2,128)(2,1)S(1)} async-done(((bf16[64,2,1280]{2,1,0:T(2,128)(2,1)}), bf16[64,2,1280]{2,1,0:T(2,128)(2,1)S(1)}, u32[]{:S(2)}, u32[]{:S(2)}) %all-to-all-start.3) | async-done | bytes 327712 | tf_op jit(solution)/shard_map/all_to_all | solution.py:34
  106.0 0.8 total.1
  (2 shorter events, 0.0 us)
Async XLA Ops:
  0.6 26.0 %copy-start.2 = (bf16[1,256,1280]{2,1,0:T(8,128)(2,1)S(1)}, bf16[1,256,1280]{2,1,0:T(8,128)(2,1)}, u32[]{:S(2)}) copy-start(bf16[1,256,1280]{2,1,0:T(8,128)(2,1)} %param.9) | copy-start | bytes 1966084
  0.6 26.0 %copy-start = (bf16[1,256,1280]{2,1,0:T(8,128)(2,1)S(1)}, bf16[1,256,1280]{2,1,0:T(8,128)(2,1)}, u32[]{:S(2)}) copy-start(bf16[1,256,1280]{2,1,0:T(8,128)(2,1)} %param.5) | copy-start | bytes 1966084
  23.1 3.6 %collective-permute-start = (bf16[64,2,1280]{2,1,0:T(2,128)(2,1)S(1)}, bf16[64,2,1280]{2,1,0:T(2,128)(2,1)S(1)}, u32[]{:S(2)}, u32[]{:S(2)}) collective-permute-start(bf16[64,2,1280]{2,1,0:T(2,128)(2,1)S(1)} %all_to_all.20.own), channel_id=1, source_target_pairs={{0,1},{1,0},{2,3},{3,2},{4,5},{5,4},{6,7},{7,6},{8,9},{9,8},{10,11... | collective-permute-start | bytes 983048 | tf_op jit(solution)/shard_map/ppermute | solution.py:38
  26.6 27.0 %slice-start = ((s8[6553600]{0:T(1024)(128)(4,1)}), s8[4194304]{0:T(1024)(128)(4,1)S(1)}, s32[]{:S(2)}) async-start(s8[6553600]{0:T(1024)(128)(4,1)} %bitcast.8), calls=%async_computation.4 | async-start | bytes 8388608
  26.6 27.0 %slice-start.2 = ((s8[6553600]{0:T(1024)(128)(4,1)}), s8[4194304]{0:T(1024)(128)(4,1)S(1)}, s32[]{:S(2)}) async-start(s8[6553600]{0:T(1024)(128)(4,1)} %bitcast.11), calls=%async_computation.6 | async-start | bytes 8388608
  26.6 26.9 %slice-start.1 = ((s8[6553600]{0:T(1024)(128)(4,1)}), s8[2359296]{0:T(1024)(128)(4,1)S(1)}, s32[]{:S(2)}) async-start(s8[6553600]{0:T(1024)(128)(4,1)} %bitcast.8), calls=%async_computation.5 | async-start | bytes 4718592
  26.7 26.9 %slice-start.3 = ((s8[6553600]{0:T(1024)(128)(4,1)}), s8[2359296]{0:T(1024)(128)(4,1)S(1)}, s32[]{:S(2)}) async-start(s8[6553600]{0:T(1024)(128)(4,1)} %bitcast.11), calls=%async_computation.7 | async-start | bytes 4718592
  60.8 26.0 %copy-start.1 = (bf16[1,256,1280]{2,1,0:T(8,128)(2,1)S(1)}, bf16[1,256,1280]{2,1,0:T(8,128)(2,1)}, u32[]{:S(2)}) copy-start(bf16[1,256,1280]{2,1,0:T(8,128)(2,1)} %param.5) | copy-start | bytes 1966084
  60.8 26.0 %copy-start.3 = (bf16[1,256,1280]{2,1,0:T(8,128)(2,1)S(1)}, bf16[1,256,1280]{2,1,0:T(8,128)(2,1)}, u32[]{:S(2)}) copy-start(bf16[1,256,1280]{2,1,0:T(8,128)(2,1)} %param.9) | copy-start | bytes 1966084
  88.3 1.7 %collective-permute-start.1 = (bf16[64,2,1280]{2,1,0:T(2,128)(2,1)S(1)}, bf16[64,2,1280]{2,1,0:T(2,128)(2,1)S(1)}, u32[]{:S(2)}, u32[]{:S(2)}) collective-permute-start(bf16[64,2,1280]{2,1,0:T(2,128)(2,1)S(1)} %get-tuple-element.28), channel_id=1, source_target_pairs={{0,1},{1,0},{2,3},{3,2},{4,5},{5,4},{6,7},{7,6},{8,9},{9,8},{10,11... | collective-permute-start | bytes 983048 | tf_op jit(solution)/shard_map/ppermute | solution.py:38
  90.7 15.2 %all-to-all-start.3 = ((bf16[64,2,1280]{2,1,0:T(2,128)(2,1)}), bf16[64,2,1280]{2,1,0:T(2,128)(2,1)S(1)}, u32[]{:S(2)}, u32[]{:S(2)}) async-start(bf16[64,2,1280]{2,1,0:T(2,128)(2,1)} %add.1), calls=%async_computation.3 | async-start | bytes 655360 | tf_op jit(solution)/shard_map/all_to_all | solution.py:34

commit v6 on v5

--- a/solution.py
+++ b/solution.py
@@ -13,7 +13,6 @@
 LOW = jnp.bfloat16
 FF_BLOCK = 512
 D_BLOCK = 256
-SEND_PARTS = 2
 MIB = 1 << 20
 
 inv_root_two = 0.7071067811865476
@@ -117,12 +116,10 @@
     combine_in,
     own,
     other,
-    grad_low_hbm,
+    grad_low,
     terms,
-    grad_low,
     slot_out,
     grad_slot_in,
-    sem,
 ):
     slot_out[...] = back[:, 0].reshape(slot_out.shape)
     grad_slot_in[...] = back[:, 1].reshape(slot_out.shape)
@@ -134,24 +131,9 @@
         grad_dispatch - jnp.sum(dispatch * grad_dispatch, axis=0, keepdims=True)
     ) + combine * (grad_combine - jnp.sum(combine * grad_combine, axis=1, keepdims=True))
     grad_low[...] = grad_logits.astype(LOW)
-    keep = pltpu.make_async_copy(grad_low, grad_low_hbm, sem)
-    keep.start()
     terms[...] = dot(grad_low[...], tokens[...], ((0,), (0,))).astype(LOW).reshape(terms.shape)
     other[...] = terms[:, CORES - 1 - core[0]]
     own[...] = terms[:, core[0]]
-    keep.wait()
-
-
-def add_kernel(own, other, sums_hbm, sums, sems):
-    some = sums.shape[0] // SEND_PARTS
-    copies = []
-    for j in range(SEND_PARTS):
-        part = pl.ds(j * some, some)
-        sums[part] = own[part] + other[part]
-        copies.append(pltpu.make_async_copy(sums.at[part], sums_hbm.at[part], sems.at[j]))
-        copies[j].start()
-    for copy in copies:
-        copy.wait()
 
 
 def finish_kernel(
@@ -159,7 +141,7 @@
     dispatch,
     combine,
     hidden,
-    grad_low_hbm,
+    grad_low,
     keys_hbm,
     grads_hbm,
     mixed_hbm,
@@ -167,7 +149,6 @@
     grad_second_hbm,
     slot_out,
     grad_slot_in,
-    grad_low,
     keys,
     grads,
     mixed_out,
@@ -176,8 +157,7 @@
     sems,
 ):
     arrivals = [
-        pltpu.make_async_copy(grad_low_hbm, grad_low, sems.at[5]),
-        pltpu.make_async_copy(keys_hbm, keys, sems.at[6]),
+        pltpu.make_async_copy(keys_hbm, keys, sems.at[5]),
         pltpu.make_async_copy(grads_hbm, grads, sems.at[0]),
     ]
     for arrival in arrivals:
@@ -189,12 +169,11 @@
     grad_slot_in[...] = back[:, 1].reshape(slot_out.shape)
     through_slots = dot(dispatch[...].astype(LOW), grad_slot_in[...], ((1,), (0,)))
     arrivals[0].wait()
-    arrivals[1].wait()
     through_keys = dot(grad_low[...], keys[...], ((1,), (0,)))
     grad_tokens[...] = (through_slots + through_keys).astype(LOW)
     leave_tokens = pltpu.make_async_copy(grad_tokens, grad_tokens_hbm, sems.at[2])
     leave_tokens.start()
-    arrivals[2].wait()
+    arrivals[1].wait()
     copies = []
     for i in range(hidden.shape[1] // FF_BLOCK):
         if i >= 2:
@@ -209,15 +188,6 @@
         copy.wait()
 
 
-def sum_kernel(terms, total):
-    pairs, each, width = terms.shape
-    owner = lax.broadcasted_iota(jnp.int32, (8, pairs * each), 0)
-    slot = lax.broadcasted_iota(jnp.int32, (8, pairs * each), 1) % each
-    chosen = jnp.where(owner == slot, 1.0, 0.0).astype(LOW)
-    flat = terms[...].reshape(pairs * each, width)
-    total[...] = dot(chosen, flat, ((1,), (0,)))[0:each]
-
-
 def spread_kernel(keys_hbm, send, keys, sem):
     copy = pltpu.make_async_copy(keys_hbm, keys, sem)
     copy.start()
@@ -237,6 +207,10 @@
 
 def stay(array):
     return pltpu.with_memory_space_constraint(array, pltpu.HBM)
+
+
+def stay_near(array):
+    return pltpu.with_memory_space_constraint(array, pltpu.VMEM)
 
 
 def shaped(dtype, *shape):
@@ -314,29 +288,19 @@
         out_shape=[
             shaped(LOW, *half_shape),
             shaped(LOW, *half_shape),
-            in_hbm(LOW, length, slots),
+            pltpu.VMEM((length, slots), LOW),
         ],
         in_specs=[SMEM] + [VMEM] * 5,
-        out_specs=[VMEM, VMEM, HBM],
+        out_specs=[VMEM] * 3,
         scratch_shapes=[
             pltpu.VMEM(quad_shape, LOW),
-            pltpu.VMEM((length, slots), LOW),
-            pltpu.VMEM((slots, width), LOW),
-            pltpu.VMEM((slots, width), LOW),
-            pltpu.SemaphoreType.DMA,
+            pltpu.VMEM((slots, width), LOW),
+            pltpu.VMEM((slots, width), LOW),
         ],
         compiler_params=pltpu.CompilerParams(vmem_limit_bytes=8 * MIB),
         name="logit",
     )(core, back, tokens, cotangent, dispatch, combine)
-    send = pl.pallas_call(
-        add_kernel,
-        out_shape=in_hbm(LOW, *half_shape),
-        in_specs=[VMEM] * 2,
-        out_specs=HBM,
-        scratch_shapes=[pltpu.VMEM(half_shape, LOW), pltpu.SemaphoreType.DMA((SEND_PARTS,))],
-        compiler_params=pltpu.CompilerParams(vmem_limit_bytes=4 * MIB),
-        name="add",
-    )(own_terms, swap_cores(other_terms))
+    send = own_terms + swap_cores(other_terms)
     terms = exchange(send, ACROSS)
     mixed_out, grad_tokens, grad_second = pl.pallas_call(
         finish_kernel,
@@ -345,30 +309,22 @@
             in_hbm(LOW, length, width),
             in_hbm(LOW, inner, width),
         ],
-        in_specs=[VMEM] * 4 + [HBM] * 3,
+        in_specs=[VMEM] * 5 + [HBM] * 2,
         out_specs=[HBM] * 3,
         scratch_shapes=[
             pltpu.VMEM((slots, width), LOW),
             pltpu.VMEM((slots, width), LOW),
-            pltpu.VMEM((length, slots), LOW),
             pltpu.VMEM((slots, width), LOW),
             pltpu.VMEM((rows, width), LOW),
             pltpu.VMEM((length, width), LOW),
             pltpu.VMEM((length, width), LOW),
             pltpu.VMEM((2, FF_BLOCK, width), LOW),
-            pltpu.SemaphoreType.DMA((7,)),
+            pltpu.SemaphoreType.DMA((6,)),
         ],
         compiler_params=pltpu.CompilerParams(vmem_limit_bytes=16 * MIB),
         name="finish",
-    )(back, dispatch, combine, hidden, stay(grad_low), stay(keys_all), stay(grads))
-    grad_keys = pl.pallas_call(
-        sum_kernel,
-        out_shape=shaped(jnp.float32, SLOTS_EXP, width),
-        in_specs=[VMEM],
-        out_specs=VMEM,
-        compiler_params=pltpu.CompilerParams(vmem_limit_bytes=4 * MIB),
-        name="total",
-    )(terms)
+    )(back, dispatch, combine, hidden, stay_near(grad_low), stay(keys_all), stay(grads))
+    grad_keys = jnp.sum(terms.astype(jnp.float32), axis=0)
     return (mixed_out[None], grad_tokens[None], grad_keys, grad_second[None])
 
 

time: 108 us -> 109 us (level)
  other arithmetic: 0.01 us -> 2.93 us
  Pallas kernels: 19.1 us -> 17.2 us
    reduce_sum x0 -> x1, other arithmetic: none -> 1.86 us  [local(): grad_keys = jnp.sum(terms.astype(jnp.float32), axis=0)]
    pallas_call x2 -> x0, Pallas kernels: 1.53 us -> none  [the longest x1 0.78 us: local(): pl.pallas_call(sum_kernel, out_shape=shaped(jnp.float32, SLOTS_EXP, width...]
where the time goes in v6:
time: 109 us; the launch traced here: 108 us
  blocking collectives  73 us (67%)
  Pallas kernels  17.2 us (16%)
  starting transfers between devices  8.03 us (7%)
  waiting for transfers between devices  6.3 us (6%)
  other arithmetic  2.93 us (3%)
    all_to_all x3, blocking collectives, exchange(): return lax.all_to_all(blocks, axes, split_axis=0, concat_axis=0, tiled=True)  73 us
    pallas_call x1, Pallas kernels, local(): pl.pallas_call(expert_kernel, out_shape=[shaped(LOW, *twin_shape), shaped...  7.16 us
    pallas_call x1, Pallas kernels, local(): pl.pallas_call(finish_kernel, out_shape=[in_hbm(LOW, length, width), in_h...  6.69 us
    all_to_all x1, starting transfers between devices, exchange(): return lax.all_to_all(blocks, axes, split_axis=0, concat_axis=0, tiled=True)  5.62 us
    all_to_all x1, waiting for transfers between devices, exchange(): return lax.all_to_all(blocks, axes, split_axis=0, concat_axis=0, tiled=True)  3.43 us
    ppermute x2, waiting for transfers between devices, swap_cores(): return lax.ppermute(block, 'core', [(0, 1), (1, 0)])  2.87 us
    ppermute x2, starting transfers between devices, swap_cores(): return lax.ppermute(block, 'core', [(0, 1), (1, 0)])  2.41 us
  transfers between devices with their start and end apart: 3, of which 3 were waited for; matrix products, arithmetic and copies ran while one was open for 0% of the time, Pallas kernels for 6%

profile of v6, /device:TPU:1, one launch (start us, length us, event | category | flops | bytes accessed | tf_op | source)
XLA Modules:
  0.0 108.3 jit_solution(10027847023372196457)
XLA Ops:
  0.6 0.0 copy-start.2
  0.6 0.0 copy-start
  0.7 0.8 spread.1
  1.5 21.6 %all_to_all.20.own = bf16[64,2,1280]{2,1,0:T(2,128)(2,1)S(1)} all-to-all(bf16[64,2,1280]{2,1,0:T(2,128)(2,1)S(1)} %spread.1), channel_id=1, replica_groups=mesh['dp'=8,'chip'=8,'core'=2] {'dp','chip'}, dimensions={0} | all-to-all | bytes 655360 | tf_op jit(solution)/shard_map/all_to_all | solution.py:33
  23.1 2.3 %collective-permute-start = (bf16[64,2,1280]{2,1,0:T(2,128)(2,1)S(1)}, bf16[64,2,1280]{2,1,0:T(2,128)(2,1)S(1)}, u32[]{:S(2)}, u32[]{:S(2)}) collective-permute-start(bf16[64,2,1280]{2,1,0:T(2,128)(2,1)S(1)} %all_to_all.20.own), channel_id=1, source_target_pairs={{0,1},{1,0},{2,3},{3,2},{4,5},{5,4},{6,7},{7,6},{8,9},{9,8},{10,11... | collective-permute-start | bytes 983048 | tf_op jit(solution)/shard_map/ppermute | solution.py:37
  25.4 1.3 %collective-permute-done.other = bf16[64,2,1280]{2,1,0:T(2,128)(2,1)S(1)} collective-permute-done((bf16[64,2,1280]{2,1,0:T(2,128)(2,1)S(1)}, bf16[64,2,1280]{2,1,0:T(2,128)(2,1)S(1)}, u32[]{:S(2)}, u32[]{:S(2)}) %collective-permute-start) | collective-permute-done | bytes 327712 | tf_op jit(solution)/shard_map/ppermute | solution.py:37
  26.6 0.0 slice-start
  26.6 0.0 slice-start.2
  26.6 0.0 copy-done.2
  26.6 0.0 copy-done
  26.6 0.0 slice-start.1
  26.7 0.0 slice-start.3
  26.7 1.4 %route.1 = (bf16[128,2,2,1280]{3,2,1,0:T(2,128)(2,1)S(1)}, f32[256,256]{1,0:T(8,128)S(1)}, f32[256,256]{1,0:T(8,128)S(1)}, bf16[256,1280]{1,0:T(8,128)(2,1)}) custom-call(s32[1]{0:T(128)} %bitcast.core, bf16[256,1280]{1,0:T(8,128)(2,1)S(1)} %bitcast.14, bf16[256,1280]{1,0:T(8,128)(2,1)S(1)} %bitcast.16, bf16[64,2,1280]{2,1,0:T(2,128)(2,1)S(1)} %all_to_all.20.own, ...), custom_call_target="tpu_custom_call" | custom-call | flops 20000000000 | bytes 1000000 | tf_op jit(solution)/shard_map/route/pallas_call | solution.py:244
  28.1 25.5 %all_to_all.21.arrived = bf16[128,2,2,1280]{3,2,1,0:T(2,128)(2,1)S(1)} all-to-all(bf16[128,2,2,1280]{3,2,1,0:T(2,128)(2,1)S(1)} %get-tuple-element.17), channel_id=1, replica_groups=mesh['dp'=8,'chip'=8,'core'=2] {'dp','chip','core'}, dimensions={0} | all-to-all | bytes 2621440 | tf_op jit(solution)/shard_map/all_to_all | solution.py:33
  53.6 0.0 slice-done
  53.6 0.0 slice-done.2
  53.6 0.0 slice-done.1
  53.6 0.0 slice-done.3
  53.6 7.2 %expert.1 = (bf16[128,2,2,1280]{3,2,1,0:T(2,128)(2,1)S(1)}, bf16[256,2560]{1,0:T(8,128)(2,1)S(1)}, bf16[256,1280]{1,0:T(8,128)(2,1)}) custom-call(bf16[128,2,2,1280]{3,2,1,0:T(2,128)(2,1)S(1)} %all_to_all.21.arrived, bf16[1280,2560]{1,0:T(8,128)(2,1)S(1)} %bitcast.10, bf16[2560,1280]{1,0:T(8,128)(2,1)S(1)} %bitcast.13), custom_call_target="tpu_custom_call" | custom-call | tf_op jit(solution)/shard_map/expert/pallas_call | solution.py:266
  60.8 0.0 copy-start.1
  60.8 0.0 copy-start.3
  60.8 26.0 %all_to_all.22.back = bf16[128,2,2,1280]{3,2,1,0:T(2,128)(2,1)S(1)} all-to-all(bf16[128,2,2,1280]{3,2,1,0:T(2,128)(2,1)S(1)} %get-tuple-element.18), channel_id=1, replica_groups=mesh['dp'=8,'chip'=8,'core'=2] {'dp','chip','core'}, dimensions={0} | all-to-all | bytes 2621440 | tf_op jit(solution)/shard_map/all_to_all | solution.py:33
  86.8 0.0 copy-done.1
  86.8 0.0 copy-done.3
  86.8 1.1 %logit.1 = (bf16[64,2,1280]{2,1,0:T(2,128)(2,1)S(1)}, bf16[64,2,1280]{2,1,0:T(2,128)(2,1)S(1)}, bf16[256,256]{1,0:T(8,128)(2,1)S(1)}) custom-call(s32[1]{0:T(128)} %bitcast.core, bf16[128,2,2,1280]{3,2,1,0:T(2,128)(2,1)S(1)} %all_to_all.22.back, bf16[256,1280]{1,0:T(8,128)(2,1)S(1)} %bitcast.15, bf16[256,1280]{1,0:T(8,128)(2,1)S(1)} %bitcast.17, ...), custom_call_target="tpu_custom_call" | custom-call | tf_op jit(solution)/shard_map/logit/pallas_call | solution.py:286
  87.9 0.1 collective-permute-start.1
  88.0 1.6 %collective-permute-done.1 = bf16[64,2,1280]{2,1,0:T(2,128)(2,1)S(1)} collective-permute-done((bf16[64,2,1280]{2,1,0:T(2,128)(2,1)S(1)}, bf16[64,2,1280]{2,1,0:T(2,128)(2,1)S(1)}, u32[]{:S(2)}, u32[]{:S(2)}) %collective-permute-start.1) | collective-permute-done | bytes 327712 | tf_op jit(solution)/shard_map/ppermute | solution.py:37
  89.7 1.1 add.3
  90.7 5.6 %all-to-all-start.3 = ((bf16[64,2,1280]{2,1,0:T(2,128)(2,1)}), bf16[64,2,1280]{2,1,0:T(2,128)(2,1)}, u32[]{:S(2)}, u32[]{:S(2)}) async-start(bf16[64,2,1280]{2,1,0:T(2,128)(2,1)} %add.3), calls=%async_computation.3 | async-start | bytes 655360 | tf_op jit(solution)/shard_map/all_to_all | solution.py:33
  96.4 6.7 %finish.1 = (bf16[256,1280]{1,0:T(8,128)(2,1)}, bf16[256,1280]{1,0:T(8,128)(2,1)}, bf16[2560,1280]{1,0:T(8,128)(2,1)}) custom-call(bf16[128,2,2,1280]{3,2,1,0:T(2,128)(2,1)S(1)} %all_to_all.22.back, f32[256,256]{1,0:T(8,128)S(1)} %get-tuple-element.19.dispatch_in.dispatch, f32[256,256]{1,0:T(8,128)S(1)} %get-tuple-element.20.combine_in.combine, ...), custom_call_target="tpu_custom_call" | custom-call | tf_op jit(solution)/shard_map/finish/pallas_call | solution.py:305
  103.0 3.4 %all-to-all-done.3 = bf16[64,2,1280]{2,1,0:T(2,128)(2,1)} async-done(((bf16[64,2,1280]{2,1,0:T(2,128)(2,1)}), bf16[64,2,1280]{2,1,0:T(2,128)(2,1)}, u32[]{:S(2)}, u32[]{:S(2)}) %all-to-all-start.3) | async-done | bytes 327712 | tf_op jit(solution)/shard_map/all_to_all | solution.py:33
  106.5 1.9 %convert_reduce_fusion = f32[2,1280]{1,0:T(2,128)} fusion(bf16[64,2,1280]{2,1,0:T(2,128)(2,1)} %all-to-all-done.3), kind=kLoop, calls=%fused_computation | loop fusion | flops 325120 | bytes 337920 | tf_op jit(solution)/shard_map/reduce_sum | solution.py:327
  (2 shorter events, 0.0 us)
Async XLA Ops:
  0.6 26.0 %copy-start.2 = (bf16[1,256,1280]{2,1,0:T(8,128)(2,1)S(1)}, bf16[1,256,1280]{2,1,0:T(8,128)(2,1)}, u32[]{:S(2)}) copy-start(bf16[1,256,1280]{2,1,0:T(8,128)(2,1)} %param.9) | copy-start | bytes 1966084
  0.6 26.0 %copy-start = (bf16[1,256,1280]{2,1,0:T(8,128)(2,1)S(1)}, bf16[1,256,1280]{2,1,0:T(8,128)(2,1)}, u32[]{:S(2)}) copy-start(bf16[1,256,1280]{2,1,0:T(8,128)(2,1)} %param.5) | copy-start | bytes 1966084
  23.1 3.6 %collective-permute-start = (bf16[64,2,1280]{2,1,0:T(2,128)(2,1)S(1)}, bf16[64,2,1280]{2,1,0:T(2,128)(2,1)S(1)}, u32[]{:S(2)}, u32[]{:S(2)}) collective-permute-start(bf16[64,2,1280]{2,1,0:T(2,128)(2,1)S(1)} %all_to_all.20.own), channel_id=1, source_target_pairs={{0,1},{1,0},{2,3},{3,2},{4,5},{5,4},{6,7},{7,6},{8,9},{9,8},{10,11... | collective-permute-start | bytes 983048 | tf_op jit(solution)/shard_map/ppermute | solution.py:37
  26.6 27.0 %slice-start = ((s8[6553600]{0:T(1024)(128)(4,1)}), s8[4194304]{0:T(1024)(128)(4,1)S(1)}, s32[]{:S(2)}) async-start(s8[6553600]{0:T(1024)(128)(4,1)} %bitcast.8), calls=%async_computation.4 | async-start | bytes 8388608
  26.6 27.0 %slice-start.2 = ((s8[6553600]{0:T(1024)(128)(4,1)}), s8[4194304]{0:T(1024)(128)(4,1)S(1)}, s32[]{:S(2)}) async-start(s8[6553600]{0:T(1024)(128)(4,1)} %bitcast.11), calls=%async_computation.6 | async-start | bytes 8388608
  26.6 26.9 %slice-start.1 = ((s8[6553600]{0:T(1024)(128)(4,1)}), s8[2359296]{0:T(1024)(128)(4,1)S(1)}, s32[]{:S(2)}) async-start(s8[6553600]{0:T(1024)(128)(4,1)} %bitcast.8), calls=%async_computation.5 | async-start | bytes 4718592
  26.7 26.9 %slice-start.3 = ((s8[6553600]{0:T(1024)(128)(4,1)}), s8[2359296]{0:T(1024)(128)(4,1)S(1)}, s32[]{:S(2)}) async-start(s8[6553600]{0:T(1024)(128)(4,1)} %bitcast.11), calls=%async_computation.7 | async-start | bytes 4718592
  60.8 26.0 %copy-start.1 = (bf16[1,256,1280]{2,1,0:T(8,128)(2,1)S(1)}, bf16[1,256,1280]{2,1,0:T(8,128)(2,1)}, u32[]{:S(2)}) copy-start(bf16[1,256,1280]{2,1,0:T(8,128)(2,1)} %param.5) | copy-start | bytes 1966084
  60.8 26.0 %copy-start.3 = (bf16[1,256,1280]{2,1,0:T(8,128)(2,1)S(1)}, bf16[1,256,1280]{2,1,0:T(8,128)(2,1)}, u32[]{:S(2)}) copy-start(bf16[1,256,1280]{2,1,0:T(8,128)(2,1)} %param.9) | copy-start | bytes 1966084
  87.9 1.7 %collective-permute-start.1 = (bf16[64,2,1280]{2,1,0:T(2,128)(2,1)S(1)}, bf16[64,2,1280]{2,1,0:T(2,128)(2,1)S(1)}, u32[]{:S(2)}, u32[]{:S(2)}) collective-permute-start(bf16[64,2,1280]{2,1,0:T(2,128)(2,1)S(1)} %get-tuple-element.28), channel_id=1, source_target_pairs={{0,1},{1,0},{2,3},{3,2},{4,5},{5,4},{6,7},{7,6},{8,9},{9,8},{10,11... | collective-permute-start | bytes 983048 | tf_op jit(solution)/shard_map/ppermute | solution.py:37
  90.7 15.8 %all-to-all-start.3 = ((bf16[64,2,1280]{2,1,0:T(2,128)(2,1)}), bf16[64,2,1280]{2,1,0:T(2,128)(2,1)}, u32[]{:S(2)}, u32[]{:S(2)}) async-start(bf16[64,2,1280]{2,1,0:T(2,128)(2,1)} %add.3), calls=%async_computation.3 | async-start | bytes 655360 | tf_op jit(solution)/shard_map/all_to_all | solution.py:33

commit v7 on v5

--- a/solution.py
+++ b/solution.py
@@ -117,12 +117,10 @@
     combine_in,
     own,
     other,
-    grad_low_hbm,
+    grad_low,
     terms,
-    grad_low,
     slot_out,
     grad_slot_in,
-    sem,
 ):
     slot_out[...] = back[:, 0].reshape(slot_out.shape)
     grad_slot_in[...] = back[:, 1].reshape(slot_out.shape)
@@ -134,22 +132,21 @@
         grad_dispatch - jnp.sum(dispatch * grad_dispatch, axis=0, keepdims=True)
     ) + combine * (grad_combine - jnp.sum(combine * grad_combine, axis=1, keepdims=True))
     grad_low[...] = grad_logits.astype(LOW)
-    keep = pltpu.make_async_copy(grad_low, grad_low_hbm, sem)
-    keep.start()
     terms[...] = dot(grad_low[...], tokens[...], ((0,), (0,))).astype(LOW).reshape(terms.shape)
     other[...] = terms[:, CORES - 1 - core[0]]
     own[...] = terms[:, core[0]]
-    keep.wait()
-
-
-def add_kernel(own, other, sums_hbm, sums, sems):
+
+
+def add_kernel(own, other, grad_low, sums_hbm, grad_low_hbm, sums, sems):
     some = sums.shape[0] // SEND_PARTS
-    copies = []
+    keep = pltpu.make_async_copy(grad_low, grad_low_hbm, sems.at[SEND_PARTS])
+    keep.start()
+    copies = [keep]
     for j in range(SEND_PARTS):
         part = pl.ds(j * some, some)
         sums[part] = own[part] + other[part]
         copies.append(pltpu.make_async_copy(sums.at[part], sums_hbm.at[part], sems.at[j]))
-        copies[j].start()
+        copies[-1].start()
     for copy in copies:
         copy.wait()
 
@@ -314,29 +311,27 @@
         out_shape=[
             shaped(LOW, *half_shape),
             shaped(LOW, *half_shape),
-            in_hbm(LOW, length, slots),
+            shaped(LOW, length, slots),
         ],
         in_specs=[SMEM] + [VMEM] * 5,
-        out_specs=[VMEM, VMEM, HBM],
+        out_specs=[VMEM] * 3,
         scratch_shapes=[
             pltpu.VMEM(quad_shape, LOW),
-            pltpu.VMEM((length, slots), LOW),
-            pltpu.VMEM((slots, width), LOW),
-            pltpu.VMEM((slots, width), LOW),
-            pltpu.SemaphoreType.DMA,
+            pltpu.VMEM((slots, width), LOW),
+            pltpu.VMEM((slots, width), LOW),
         ],
         compiler_params=pltpu.CompilerParams(vmem_limit_bytes=8 * MIB),
         name="logit",
     )(core, back, tokens, cotangent, dispatch, combine)
-    send = pl.pallas_call(
+    send, grad_low = pl.pallas_call(
         add_kernel,
-        out_shape=in_hbm(LOW, *half_shape),
-        in_specs=[VMEM] * 2,
-        out_specs=HBM,
-        scratch_shapes=[pltpu.VMEM(half_shape, LOW), pltpu.SemaphoreType.DMA((SEND_PARTS,))],
+        out_shape=[in_hbm(LOW, *half_shape), in_hbm(LOW, length, slots)],
+        in_specs=[VMEM] * 3,
+        out_specs=[HBM] * 2,
+        scratch_shapes=[pltpu.VMEM(half_shape, LOW), pltpu.SemaphoreType.DMA((SEND_PARTS + 1,))],
         compiler_params=pltpu.CompilerParams(vmem_limit_bytes=4 * MIB),
         name="add",
-    )(own_terms, swap_cores(other_terms))
+    )(own_terms, swap_cores(other_terms), grad_low)
     terms = exchange(send, ACROSS)
     mixed_out, grad_tokens, grad_second = pl.pallas_call(
         finish_kernel,

time: 108 us -> 107 us (level)
  no operation moved by 1% of the time
where the time goes in v7:
time: 107 us; the launch traced here: 106 us
  blocking collectives  73 us (68%)
  Pallas kernels  18.9 us (18%)
  starting transfers between devices  7.48 us (7%)
  waiting for transfers between devices  6.24 us (6%)
    all_to_all x3, blocking collectives, exchange(): return lax.all_to_all(blocks, axes, split_axis=0, concat_axis=0, tiled=True)  73 us
    pallas_call x1, Pallas kernels, local(): pl.pallas_call(expert_kernel, out_shape=[shaped(LOW, *twin_shape), shaped...  7.16 us
    pallas_call x1, Pallas kernels, local(): pl.pallas_call(finish_kernel, out_shape=[in_hbm(LOW, length, width), in_h...  6.77 us
    all_to_all x1, starting transfers between devices, exchange(): return lax.all_to_all(blocks, axes, split_axis=0, concat_axis=0, tiled=True)  5.08 us
    all_to_all x1, waiting for transfers between devices, exchange(): return lax.all_to_all(blocks, axes, split_axis=0, concat_axis=0, tiled=True)  3.37 us
    ppermute x2, waiting for transfers between devices, swap_cores(): return lax.ppermute(block, 'core', [(0, 1), (1, 0)])  2.87 us
    ppermute x2, starting transfers between devices, swap_cores(): return lax.ppermute(block, 'core', [(0, 1), (1, 0)])  2.41 us
  transfers between devices with their start and end apart: 3, of which 3 were waited for; matrix products, arithmetic and copies ran while one was open for 0% of the time, Pallas kernels for 6%

profile of v7, /device:TPU:1, one launch (start us, length us, event | category | flops | bytes accessed | tf_op | source)
XLA Modules:
  0.0 106.5 jit_solution(7553582402952197569)
XLA Ops:
  0.6 0.0 copy-start.2
  0.6 0.0 copy-start
  0.7 0.8 spread.1
  1.5 21.6 %all_to_all.20.own = bf16[64,2,1280]{2,1,0:T(2,128)(2,1)S(1)} all-to-all(bf16[64,2,1280]{2,1,0:T(2,128)(2,1)S(1)} %spread.1), channel_id=1, replica_groups=mesh['dp'=8,'chip'=8,'core'=2] {'dp','chip'}, dimensions={0} | all-to-all | bytes 655360 | tf_op jit(solution)/shard_map/all_to_all | solution.py:34
  23.1 2.3 %collective-permute-start = (bf16[64,2,1280]{2,1,0:T(2,128)(2,1)S(1)}, bf16[64,2,1280]{2,1,0:T(2,128)(2,1)S(1)}, u32[]{:S(2)}, u32[]{:S(2)}) collective-permute-start(bf16[64,2,1280]{2,1,0:T(2,128)(2,1)S(1)} %all_to_all.20.own), channel_id=1, source_target_pairs={{0,1},{1,0},{2,3},{3,2},{4,5},{5,4},{6,7},{7,6},{8,9},{9,8},{10,11... | collective-permute-start | bytes 983048 | tf_op jit(solution)/shard_map/ppermute | solution.py:38
  25.4 1.3 %collective-permute-done.other = bf16[64,2,1280]{2,1,0:T(2,128)(2,1)S(1)} collective-permute-done((bf16[64,2,1280]{2,1,0:T(2,128)(2,1)S(1)}, bf16[64,2,1280]{2,1,0:T(2,128)(2,1)S(1)}, u32[]{:S(2)}, u32[]{:S(2)}) %collective-permute-start) | collective-permute-done | bytes 327712 | tf_op jit(solution)/shard_map/ppermute | solution.py:38
  26.6 0.0 slice-start
  26.6 0.0 slice-start.2
  26.6 0.0 copy-done.2
  26.6 0.0 copy-done
  26.6 0.0 slice-start.1
  26.7 0.0 slice-start.3
  26.7 1.4 %route.1 = (bf16[128,2,2,1280]{3,2,1,0:T(2,128)(2,1)S(1)}, f32[256,256]{1,0:T(8,128)S(1)}, f32[256,256]{1,0:T(8,128)S(1)}, bf16[256,1280]{1,0:T(8,128)(2,1)}) custom-call(s32[1]{0:T(128)} %bitcast.core, bf16[256,1280]{1,0:T(8,128)(2,1)S(1)} %bitcast.14, bf16[256,1280]{1,0:T(8,128)(2,1)S(1)} %bitcast.16, bf16[64,2,1280]{2,1,0:T(2,128)(2,1)S(1)} %all_to_all.20.own, ...), custom_call_target="tpu_custom_call" | custom-call | flops 20000000000 | bytes 1000000 | tf_op jit(solution)/shard_map/route/pallas_call | solution.py:267
  28.1 25.5 %all_to_all.21.arrived = bf16[128,2,2,1280]{3,2,1,0:T(2,128)(2,1)S(1)} all-to-all(bf16[128,2,2,1280]{3,2,1,0:T(2,128)(2,1)S(1)} %get-tuple-element.19), channel_id=1, replica_groups=mesh['dp'=8,'chip'=8,'core'=2] {'dp','chip','core'}, dimensions={0} | all-to-all | bytes 2621440 | tf_op jit(solution)/shard_map/all_to_all | solution.py:34
  53.6 0.0 slice-done
  53.6 0.0 slice-done.2
  53.6 0.0 slice-done.1
  53.6 0.0 slice-done.3
  53.6 7.2 %expert.1 = (bf16[128,2,2,1280]{3,2,1,0:T(2,128)(2,1)S(1)}, bf16[256,2560]{1,0:T(8,128)(2,1)S(1)}, bf16[256,1280]{1,0:T(8,128)(2,1)}) custom-call(bf16[128,2,2,1280]{3,2,1,0:T(2,128)(2,1)S(1)} %all_to_all.21.arrived, bf16[1280,2560]{1,0:T(8,128)(2,1)S(1)} %bitcast.10, bf16[2560,1280]{1,0:T(8,128)(2,1)S(1)} %bitcast.13), custom_call_target="tpu_custom_call" | custom-call | tf_op jit(solution)/shard_map/expert/pallas_call | solution.py:289
  60.8 0.0 copy-start.1
  60.8 0.0 copy-start.3
  60.8 26.0 %all_to_all.22.back = bf16[128,2,2,1280]{3,2,1,0:T(2,128)(2,1)S(1)} all-to-all(bf16[128,2,2,1280]{3,2,1,0:T(2,128)(2,1)S(1)} %get-tuple-element.20), channel_id=1, replica_groups=mesh['dp'=8,'chip'=8,'core'=2] {'dp','chip','core'}, dimensions={0} | all-to-all | bytes 2621440 | tf_op jit(solution)/shard_map/all_to_all | solution.py:34
  86.8 0.0 copy-done.1
  86.8 0.0 copy-done.3
  86.8 1.1 %logit.1 = (bf16[64,2,1280]{2,1,0:T(2,128)(2,1)S(1)}, bf16[64,2,1280]{2,1,0:T(2,128)(2,1)S(1)}, bf16[256,256]{1,0:T(8,128)(2,1)S(1)}) custom-call(s32[1]{0:T(128)} %bitcast.core, bf16[128,2,2,1280]{3,2,1,0:T(2,128)(2,1)S(1)} %all_to_all.22.back, bf16[256,1280]{1,0:T(8,128)(2,1)S(1)} %bitcast.15, bf16[256,1280]{1,0:T(8,128)(2,1)S(1)} %bitcast.17, ...), custom_call_target="tpu_custom_call" | custom-call | tf_op jit(solution)/shard_map/logit/pallas_call | solution.py:309
  87.9 0.1 collective-permute-start.1
  88.0 1.6 %collective-permute-done.1.other = bf16[64,2,1280]{2,1,0:T(2,128)(2,1)S(1)} collective-permute-done((bf16[64,2,1280]{2,1,0:T(2,128)(2,1)S(1)}, bf16[64,2,1280]{2,1,0:T(2,128)(2,1)S(1)}, u32[]{:S(2)}, u32[]{:S(2)}) %collective-permute-start.1) | collective-permute-done | bytes 327712 | tf_op jit(solution)/shard_map/ppermute | solution.py:38
  89.7 0.8 add.1
  90.5 5.1 %all-to-all-start.3 = ((bf16[64,2,1280]{2,1,0:T(2,128)(2,1)}), bf16[64,2,1280]{2,1,0:T(2,128)(2,1)S(1)}, u32[]{:S(2)}, u32[]{:S(2)}) async-start(bf16[64,2,1280]{2,1,0:T(2,128)(2,1)} %get-tuple-element.32), calls=%async_computation.3 | async-start | bytes 655360 | tf_op jit(solution)/shard_map/all_to_all | solution.py:34
  95.5 6.8 %finish.1 = (bf16[256,1280]{1,0:T(8,128)(2,1)}, bf16[256,1280]{1,0:T(8,128)(2,1)}, bf16[2560,1280]{1,0:T(8,128)(2,1)}) custom-call(bf16[128,2,2,1280]{3,2,1,0:T(2,128)(2,1)S(1)} %all_to_all.22.back, f32[256,256]{1,0:T(8,128)S(1)} %get-tuple-element.21.dispatch_in.dispatch, f32[256,256]{1,0:T(8,128)S(1)} %get-tuple-element.22.combine_in.combine, ...), custom_call_target="tpu_custom_call" | custom-call | tf_op jit(solution)/shard_map/finish/pallas_call | solution.py:336
  102.3 3.4 %all-to-all-done.3.terms = bf16[64,2,1280]{2,1,0:T(2,128)(2,1)S(1)} async-done(((bf16[64,2,1280]{2,1,0:T(2,128)(2,1)}), bf16[64,2,1280]{2,1,0:T(2,128)(2,1)S(1)}, u32[]{:S(2)}, u32[]{:S(2)}) %all-to-all-start.3) | async-done | bytes 327712 | tf_op jit(solution)/shard_map/all_to_all | solution.py:34
  105.7 0.8 total.1
  (2 shorter events, 0.0 us)
Async XLA Ops:
  0.6 26.0 %copy-start.2 = (bf16[1,256,1280]{2,1,0:T(8,128)(2,1)S(1)}, bf16[1,256,1280]{2,1,0:T(8,128)(2,1)}, u32[]{:S(2)}) copy-start(bf16[1,256,1280]{2,1,0:T(8,128)(2,1)} %param.9) | copy-start | bytes 1966084
  0.6 26.0 %copy-start = (bf16[1,256,1280]{2,1,0:T(8,128)(2,1)S(1)}, bf16[1,256,1280]{2,1,0:T(8,128)(2,1)}, u32[]{:S(2)}) copy-start(bf16[1,256,1280]{2,1,0:T(8,128)(2,1)} %param.5) | copy-start | bytes 1966084
  23.1 3.6 %collective-permute-start = (bf16[64,2,1280]{2,1,0:T(2,128)(2,1)S(1)}, bf16[64,2,1280]{2,1,0:T(2,128)(2,1)S(1)}, u32[]{:S(2)}, u32[]{:S(2)}) collective-permute-start(bf16[64,2,1280]{2,1,0:T(2,128)(2,1)S(1)} %all_to_all.20.own), channel_id=1, source_target_pairs={{0,1},{1,0},{2,3},{3,2},{4,5},{5,4},{6,7},{7,6},{8,9},{9,8},{10,11... | collective-permute-start | bytes 983048 | tf_op jit(solution)/shard_map/ppermute | solution.py:38
  26.6 27.0 %slice-start = ((s8[6553600]{0:T(1024)(128)(4,1)}), s8[4194304]{0:T(1024)(128)(4,1)S(1)}, s32[]{:S(2)}) async-start(s8[6553600]{0:T(1024)(128)(4,1)} %bitcast.8), calls=%async_computation.4 | async-start | bytes 8388608
  26.6 27.0 %slice-start.2 = ((s8[6553600]{0:T(1024)(128)(4,1)}), s8[4194304]{0:T(1024)(128)(4,1)S(1)}, s32[]{:S(2)}) async-start(s8[6553600]{0:T(1024)(128)(4,1)} %bitcast.11), calls=%async_computation.6 | async-start | bytes 8388608
  26.6 26.9 %slice-start.1 = ((s8[6553600]{0:T(1024)(128)(4,1)}), s8[2359296]{0:T(1024)(128)(4,1)S(1)}, s32[]{:S(2)}) async-start(s8[6553600]{0:T(1024)(128)(4,1)} %bitcast.8), calls=%async_computation.5 | async-start | bytes 4718592
  26.7 26.9 %slice-start.3 = ((s8[6553600]{0:T(1024)(128)(4,1)}), s8[2359296]{0:T(1024)(128)(4,1)S(1)}, s32[]{:S(2)}) async-start(s8[6553600]{0:T(1024)(128)(4,1)} %bitcast.11), calls=%async_computation.7 | async-start | bytes 4718592
  60.8 26.0 %copy-start.1 = (bf16[1,256,1280]{2,1,0:T(8,128)(2,1)S(1)}, bf16[1,256,1280]{2,1,0:T(8,128)(2,1)}, u32[]{:S(2)}) copy-start(bf16[1,256,1280]{2,1,0:T(8,128)(2,1)} %param.5) | copy-start | bytes 1966084
  60.8 26.0 %copy-start.3 = (bf16[1,256,1280]{2,1,0:T(8,128)(2,1)S(1)}, bf16[1,256,1280]{2,1,0:T(8,128)(2,1)}, u32[]{:S(2)}) copy-start(bf16[1,256,1280]{2,1,0:T(8,128)(2,1)} %param.9) | copy-start | bytes 1966084
  87.9 1.7 %collective-permute-start.1 = (bf16[64,2,1280]{2,1,0:T(2,128)(2,1)S(1)}, bf16[64,2,1280]{2,1,0:T(2,128)(2,1)S(1)}, u32[]{:S(2)}, u32[]{:S(2)}) collective-permute-start(bf16[64,2,1280]{2,1,0:T(2,128)(2,1)S(1)} %get-tuple-element.25), channel_id=1, source_target_pairs={{0,1},{1,0},{2,3},{3,2},{4,5},{5,4},{6,7},{7,6},{8,9},{9,8},{10,11... | collective-permute-start | bytes 983048 | tf_op jit(solution)/shard_map/ppermute | solution.py:38
  90.5 15.2 %all-to-all-start.3 = ((bf16[64,2,1280]{2,1,0:T(2,128)(2,1)}), bf16[64,2,1280]{2,1,0:T(2,128)(2,1)S(1)}, u32[]{:S(2)}, u32[]{:S(2)}) async-start(bf16[64,2,1280]{2,1,0:T(2,128)(2,1)} %get-tuple-element.32), calls=%async_computation.3 | async-start | bytes 655360 | tf_op jit(solution)/shard_map/all_to_all | solution.py:34
